TPU v7x, 32 devices: a whole 2x2x4 slice. The times are simulated.
32 devices in a mesh: dp: 4 (over y, core), mp: 8 (over z, x).
Axes of the slice: x: 2, y: 2, z: 4, core: 2. Of those that a mesh axis runs over, the one named last changes fastest.
Arguments:
- features: bfloat16 [4096, 65536], P('dp', 'mp'), may hold values from -6 to 6
- cotangent: bfloat16 [4096, 65536], P('dp', 'mp'), may hold values from -6 to 6
- factor_one: bfloat16 [256, 256, 256], P('mp', 'dp'), may hold values from -0.375 to 0.375
- factor_two: bfloat16 [256, 256, 256], P('mp', 'dp'), may hold values from -0.375 to 0.375
Outputs:
- layer_out: bfloat16 [4096, 65536], P('dp', 'mp')
- grad_input: bfloat16 [4096, 65536], P('dp', 'mp')
- grad_one: float32 [256, 256, 256], P('mp', 'dp')
- grad_two: float32 [256, 256, 256], P('mp', 'dp')
All inputs are finite; a program needn't handle non-finite values.
Results may differ from a plain program's by a relative error of at most 0.0095.
Values may be sent and summed in bfloat16 or wider, within the bound.
No kernel may reach another device: no remote copies, remote signals or barrier semaphores. Data moves between devices by JAX's collectives and lax.ppermute only.
A program may use at most 256 MiB of HBM per device.

v0:
```python
import functools
import math

import jax
import jax.numpy as jnp
from jax import lax
from jax.experimental import pallas as pl
from jax.experimental.pallas import tpu as pltpu
from jax.sharding import PartitionSpec as P

LANES = 128
VMEM_LIMIT = 60 * 1024 * 1024
GELU_SCALE = math.sqrt(2.0 / math.pi)


def contract(left, right, left_axis, right_axis):
    return lax.dot_general(
        left, right, (((left_axis,), (right_axis,)), ((), ())), preferred_element_type=jnp.float32
    )


def first_rows(feat_ref, weight, out_refs, unit, cuts, owners, held, swap):
    tokens = feat_ref.shape[0]
    group, width, _ = weight.shape
    for b in range(group):
        rows = contract(weight[b], feat_ref[:, b * width : (b + 1) * width], 1, 1)
        for lane in range(tokens // LANES):
            swap[lane, pl.ds(b, width, stride=group), :] = rows[
                :, lane * LANES : (lane + 1) * LANES
            ]
    for out_ref, (low, high) in zip(out_refs, cuts):
        for owner in range(owners):
            start = (owner * held + low) * group
            for lane in range(tokens // LANES):
                block = swap[lane, pl.ds(start, (high - low) * group), :]
                out_ref[owner, unit, :, :, lane * LANES : (lane + 1) * LANES] = block.reshape(
                    high - low, group, LANES
                ).astype(jnp.bfloat16)


def first_kernel(cuts, owners, held, units, *refs):
    feat_refs, w_refs, out_refs = refs[:units], refs[units : 2 * units], refs[2 * units : -2]
    weight, swap = refs[-2:]

    @pl.when(pl.program_id(0) == 0)
    def _():
        for unit, w_ref in enumerate(w_refs):
            for b in range(w_ref.shape[0]):
                weight[unit, b] = w_ref[b].T

    for unit in range(units):
        first_rows(feat_refs[unit], weight.at[unit], out_refs, unit, cuts, owners, held, swap)


def head_kernel(cuts, owners, held, shares, position_ref, feat_ref, *refs):
    part_refs, gathered, weight, swap = refs[:shares], *refs[-3:]
    rows = weight.shape[1] // shares

    @pl.when(pl.program_id(0) == 0)
    def _():
        for step, part_ref in enumerate(part_refs):
            start = pl.multiple_of((position_ref[0] ^ step) * rows, rows)
            gathered[:, pl.ds(start, rows), :] = part_ref[...]
        for b in range(weight.shape[0]):
            weight[b] = gathered[b].T

    first_rows(feat_ref, weight, refs[shares:-3], 0, cuts, owners, held, swap)


def first_call(features, group, width, cuts, owners, begin, units):
    tokens = features.shape[0]
    tile = min(256, tokens)
    outs = [
        jax.ShapeDtypeStruct((owners, units, high - low, group, tokens), jnp.bfloat16)
        for low, high in cuts
    ]
    moved = 2 * units * (tokens * group * width + group * width * width)
    moved += sum(2 * math.prod(out.shape) for out in outs)
    feat_specs = [
        pl.BlockSpec((tile, group * width), functools.partial(lambda u, t, *_: (t, u), begin + u))
        for u in range(units)
    ]
    out_specs = [
        pl.BlockSpec((owners, units, high - low, group, tile), lambda t, *_: (0, 0, 0, 0, t))
        for low, high in cuts
    ]
    swap = pltpu.VMEM((tile // LANES, width * group, LANES), jnp.float32)
    params = dict(
        out_shape=outs,
        compiler_params=pltpu.CompilerParams(vmem_limit_bytes=VMEM_LIMIT),
        cost_estimate=pl.CostEstimate(
            flops=2 * units * tokens * group * width * width,
            bytes_accessed=moved,
            transcendentals=0,
        ),
        name="first",
    )
    return (tokens // tile,), feat_specs, out_specs, swap, params


def first_parts(features, w_one, group, cuts, owners, held, begin, units):
    width = w_one.shape[1]
    grid, feat_specs, out_specs, swap, params = first_call(
        features, group, width, cuts, owners, begin, units
    )
    w_specs = [
        pl.BlockSpec((group, width, width), functools.partial(lambda u, t: (u, 0, 0), begin + u))
        for u in range(units)
    ]
    return pl.pallas_call(
        functools.partial(first_kernel, cuts, owners, held, units),
        grid=grid,
        in_specs=feat_specs + w_specs,
        out_specs=out_specs,
        scratch_shapes=[pltpu.VMEM((units, group, width, width), jnp.bfloat16), swap],
        **params,
    )(*[features] * units, *[w_one] * units)


def first_head(position, features, parts, cuts, owners, held):
    group, rows, width = parts[0].shape
    shares = len(parts)
    grid, feat_specs, out_specs, swap, params = first_call(
        features, group, width, cuts, owners, 0, 1
    )
    return pl.pallas_call(
        functools.partial(head_kernel, cuts, owners, held, shares),
        grid_spec=pltpu.PrefetchScalarGridSpec(
            num_scalar_prefetch=1,
            grid=grid,
            in_specs=feat_specs
            + [pl.BlockSpec((group, rows, width), lambda t, _: (0, 0, 0))] * shares,
            out_specs=out_specs,
            scratch_shapes=[pltpu.VMEM((group, width, width), jnp.bfloat16)] * 2 + [swap],
        ),
        **params,
    )(position, features, *parts)


def middle_kernel(owners, group, sources, backs, tile, chained, *refs):
    r_refs = refs[: len(sources)]
    w_ref, feat_ref, cot_ref = refs[len(sources) : len(sources) + 3]
    outs = refs[len(sources) + 3 + chained :]
    layer_ref, part_ref, back_refs = outs[0], outs[1], outs[2:]
    weight = w_ref[0]
    tokens = feat_ref.shape[0]
    depth = weight.shape[0]
    part = None
    for begin in range(0, tokens, tile):
        span = slice(begin, begin + tile)
        first = jnp.concatenate(
            [
                ref[:, unit, 0, :, span].astype(jnp.float32)
                for ref, units in zip(r_refs, sources)
                for unit in range(units)
            ],
            axis=1,
        )
        first = first.reshape(depth, tile).astype(jnp.bfloat16)
        value = contract(first, weight, 0, 0)
        square = value * value
        tangent = jnp.tanh(GELU_SCALE * (value + 0.044715 * square * value))
        half = 0.5 * (1.0 + tangent)
        layer_ref[span, :] = (feat_ref[span, :].astype(jnp.float32) + value * half).astype(
            jnp.bfloat16
        )
        rate = half + 0.5 * value * (1.0 - tangent * tangent) * GELU_SCALE * (
            1.0 + 3.0 * 0.044715 * square
        )
        slope = (cot_ref[span, :].astype(jnp.float32) * rate).astype(jnp.bfloat16)
        back = contract(weight, slope, 1, 1).reshape(owners, depth // owners, tile)
        start = 0
        for units, back_ref in zip(backs, back_refs):
            for unit in range(units):
                back_ref[:, unit, 0, :, span] = back[:, start : start + group].astype(jnp.bfloat16)
                start += group
        term = contract(first, slope, 1, 0)
        part = term if part is None else part + term
    part_ref[0] = part.astype(jnp.bfloat16)


def middle_part(received, w_two, features, cotangent, layer, low, high, backs):
    tokens, columns = features.shape
    owners, _, _, group, _ = received[0][0].shape
    count = high - low
    depth, width = w_two.shape[1:]
    tile = min(256, tokens)
    chained = 0 if layer is None else 1
    column = pl.BlockSpec((tokens, width), lambda j: (0, low + j))
    sources = [array.shape[1] for array, _ in received]
    operands = [array for array, _ in received] + [w_two, features, cotangent]
    operands += [layer] if chained else []

    def spec(units, skipped):
        return pl.BlockSpec(
            (owners, units, 1, group, tokens), lambda j: (0, 0, low - skipped + j, 0, 0)
        )

    return pl.pallas_call(
        functools.partial(middle_kernel, owners, group, sources, backs, tile, chained),
        grid=(count,),
        in_specs=[spec(array.shape[1], skipped) for array, skipped in received]
        + [pl.BlockSpec((1, depth, width), lambda j: (low + j, 0, 0)), column, column]
        + [pl.BlockSpec(memory_space=pl.ANY)] * chained,
        out_specs=[column, pl.BlockSpec((1, depth, width), lambda j: (j, 0, 0))]
        + [spec(units, low) for units in backs],
        out_shape=[
            jax.ShapeDtypeStruct((tokens, columns), jnp.bfloat16),
            jax.ShapeDtypeStruct((count, depth, width), jnp.bfloat16),
        ]
        + [
            jax.ShapeDtypeStruct((owners, units, count, group, tokens), jnp.bfloat16)
            for units in backs
        ],
        input_output_aliases={len(operands) - 1: 0} if chained else {},
        compiler_params=pltpu.CompilerParams(vmem_limit_bytes=VMEM_LIMIT),
        cost_estimate=pl.CostEstimate(
            flops=6 * count * tokens * depth * width,
            bytes_accessed=count * (10 * tokens * width + 4 * depth * width),
            transcendentals=count * tokens * width,
        ),
        name="middle",
    )(*operands)


def last_kernel(held, sources, shares, rows_out, grad_out, chained, position_ref, *refs):
    q_refs, refs = refs[: len(sources)], list(refs[len(sources) :])
    feat_ref = refs.pop(0) if rows_out else None
    w_ref, cot_ref = (refs.pop(0), refs.pop(0)) if grad_out else (None, None)
    refs = refs[chained:]
    keep_ref, send_ref = (refs.pop(0), refs.pop(0)) if rows_out else (None, None)
    grad_ref = refs.pop(0) if grad_out else None
    swap = refs.pop(0)
    total = refs.pop(0) if rows_out else None
    group, tokens = q_refs[0].shape[3:]
    width = swap.shape[1] // group
    lanes = tokens // LANES
    step = pl.program_id(0)

    if rows_out:

        @pl.when(step == 0)
        def _():
            total[...] = jnp.zeros_like(total)

    for q_ref, (low, high) in zip(q_refs, sources):
        for owner in range(q_ref.shape[0]):
            start = (owner * held + low) * group
            for lane in range(lanes):
                block = q_ref[owner, 0, :, :, lane * LANES : (lane + 1) * LANES]
                swap[lane, pl.ds(start, (high - low) * group), :] = block.astype(
                    jnp.float32
                ).reshape((high - low) * group, LANES)
    for b in range(group):
        back = jnp.concatenate(
            [swap[lane, pl.ds(b, width, stride=group), :] for lane in range(lanes)], axis=1
        ).astype(jnp.bfloat16)
        columns = slice(b * width, (b + 1) * width)
        if grad_out:
            through = contract(back, w_ref[b], 0, 1)
            grad_ref[:, columns] = (cot_ref[:, columns].astype(jnp.float32) + through).astype(
                jnp.bfloat16
            )
        if rows_out:
            total[b] += contract(back, feat_ref[:, columns], 1, 0)

    if rows_out:

        @pl.when(step == pl.num_programs(0) - 1)
        def _():
            rows = width // shares
            me = position_ref[0]
            for b in range(group):
                part = total[b].T.astype(jnp.bfloat16)
                for share in range(shares):
                    mine = (me & 1) == (share & 1)
                    place = (me >> 1) ^ (share >> 1)
                    block = part[share * rows : (share + 1) * rows]

                    @pl.when(mine)
                    def _():
                        keep_ref[place, b] = block

                    @pl.when(jnp.logical_not(mine))
                    def _():
                        send_ref[place, b] = block


def last_part(position, returned, unit, rows_of, grad_of, grad, shares):
    tokens = returned[0][0].shape[-1]
    owners, _, _, group, _ = returned[0][0].shape
    held = sum(array.shape[2] for array, _ in returned)
    width = owners * held
    tile = min(256, tokens)
    strip = pl.BlockSpec((tile, group * width), lambda t, _: (t, unit))
    operands, specs, sources, low = [], [], [], 0
    for array, at in returned:
        count = array.shape[2]
        index_map = functools.partial(lambda at, t, _: (0, at, 0, 0, t), at)
        operands.append(array)
        specs.append(pl.BlockSpec((owners, 1, count, group, tile), index_map))
        sources.append((low, low + count))
        low += count
    outs, out_specs, aliases = [], [], {}
    scratch = [pltpu.VMEM((tile // LANES, width * group, LANES), jnp.float32)]
    chained = 1 if grad_of is not None and grad is not None else 0
    if rows_of is not None:
        operands.append(rows_of)
        specs.append(strip)
        block = (shares // 2, group, width // shares, width)
        outs += [jax.ShapeDtypeStruct(block, jnp.bfloat16)] * 2
        out_specs += [pl.BlockSpec(block, lambda t, _: (0, 0, 0, 0))] * 2
        scratch.append(pltpu.VMEM((group, width, width), jnp.float32))
    if grad_of is not None:
        w_one, cotangent = grad_of
        operands += [w_one, cotangent]
        specs += [pl.BlockSpec((group, width, width), lambda t, _: (unit, 0, 0)), strip]
        if chained:
            operands.append(grad)
            specs.append(pl.BlockSpec(memory_space=pl.ANY))
            aliases = {len(operands): len(outs)}
        outs.append(jax.ShapeDtypeStruct(cotangent.shape, jnp.bfloat16))
        out_specs.append(strip)
    jobs = (rows_of is not None) + (grad_of is not None)
    return pl.pallas_call(
        functools.partial(
            last_kernel, held, sources, shares, rows_of is not None, grad_of is not None, chained
        ),
        grid_spec=pltpu.PrefetchScalarGridSpec(
            num_scalar_prefetch=1,
            grid=(tokens // tile,),
            in_specs=specs,
            out_specs=out_specs,
            scratch_shapes=scratch,
        ),
        out_shape=outs,
        input_output_aliases=aliases,
        compiler_params=pltpu.CompilerParams(vmem_limit_bytes=VMEM_LIMIT),
        cost_estimate=pl.CostEstimate(
            flops=2 * jobs * group * tokens * width * width,
            bytes_accessed=group * (2 + 3 * jobs) * tokens * width,
            transcendentals=0,
        ),
        name="last",
    )(position, *operands)


def exchange(array, before=None):
    if before is not None:
        array = after(array, before)
    return lax.all_to_all(array, "mp", split_axis=0, concat_axis=0, tiled=True)


def after(array, before):
    return lax.optimization_barrier((array, before))[0]


def swap_with(array, step):
    size = lax.axis_size("dp")
    return lax.ppermute(array, "dp", [(d, d ^ step) for d in range(size)])


def gathered_parts(part):
    parts = [part]
    step = lax.axis_size("dp") // 2
    while step:
        came = [swap_with(array, step) for array in parts]
        parts = [array for pair in zip(parts, came) for array in pair]
        step //= 2
    return parts


def first_hop(keep, send):
    return keep.astype(jnp.float32) + swap_with(send, 1).astype(jnp.float32)


def other_hops(totals):
    total = jnp.concatenate(totals, axis=1)
    count = total.shape[0]
    while count > 1:
        count //= 2
        came = swap_with(total[count:].astype(jnp.bfloat16), 2 * count)
        total = total[:count] + came.astype(jnp.float32)
    return total[0]


def scatter(part):
    return lax.psum_scatter(part, "dp", scatter_dimension=1, tiled=True)


def on_device(features, cotangent, factor_one, factor_two):
    owners = lax.axis_size("mp")
    shares = lax.axis_size("dp")
    held = factor_one.shape[0]
    half = held // 2
    unit = 8 if held % 16 == 0 else held
    units = held // unit

    position = jnp.full((1,), lax.axis_index("dp"), jnp.int32)
    parts = gathered_parts(factor_one[:unit])
    (head,) = first_head(position, features, parts, [(0, held)], owners, held)
    w_one = lax.all_gather(after(factor_one, head), "dp", axis=1, tiled=True)
    w_two = lax.all_gather(after(factor_two, w_one), "dp", axis=1, tiled=True)
    latest = arrived = exchange(head)
    received = [[(arrived, 0)], [(arrived, 0)]]
    if units > 1:
        cuts = [(0, half), (half, held)]
        rest = first_parts(
            after(features, head), w_one, unit, cuts, owners, held, 1, units - 1
        )
        for index, array in enumerate(rest):
            latest = exchange(array, latest)
            received[index].append((latest, index * half))

    backs = [units - 1, 1] if units > 1 else [1]
    layer, part_low, back_low = middle_part(
        received[0], w_two, features, cotangent, None, 0, half, [units]
    )
    latest = back_low = exchange(back_low, latest)
    layer, part_high, *back_high = middle_part(
        received[1], w_two, features, cotangent, layer, half, held, backs
    )
    parts_two = [scatter(part_low), scatter(part_high)]
    for index, array in enumerate(back_high):
        before = (latest, parts_two) if index else latest
        latest = back_high[index] = exchange(array, before)

    grad, hops, parts_one = None, [], []
    for index in range(units):
        final = units > 1 and index == units - 1
        back, at = (back_high[1], 0) if final else (back_high[0], index)
        if final:
            back = after(back, parts_one)
        returned = [(back_low, index), (back, at)]
        grad_of = (w_one, cotangent)
        if final:
            keep, send = last_part(position, returned, index, features, None, None, shares)
            (grad,) = last_part(position, returned, index, None, grad_of, grad, shares)
        else:
            keep, send, grad = last_part(
                position, returned, index, features, grad_of, grad, shares
            )
        hops.append(first_hop(keep, send))
        if index == units // 2 - 1 or index == units - 1:
            parts_one.append(other_hops(hops[-(units // 2 or 1) :]))
    parts_two = after(parts_two, hops[-1])
    grad_one = jnp.concatenate(parts_one[:-1] + [jnp.zeros_like(parts_one[-1])], axis=0)
    start = held - parts_one[-1].shape[0]
    grad_one = lax.dynamic_update_slice(grad_one, parts_one[-1], (start, 0, 0))
    return (
        layer,
        grad,
        grad_one,
        jnp.concatenate(parts_two, axis=0).astype(jnp.float32),
    )


def solution(mesh):
    in_specs = (P("dp", "mp"), P("dp", "mp"), P("mp", "dp", None), P("mp", "dp", None))
    out_specs = (P("dp", "mp"), P("dp", "mp"), P("mp", "dp", None), P("mp", "dp", None))
    return jax.shard_map(
        on_device, mesh=mesh, in_specs=in_specs, out_specs=out_specs, check_vma=False
    )
```

profile of v0, /device:TPU:0, one launch (start us, length us, event | category | flops | bytes accessed | tf_op | source)
XLA Modules:
  0.0 826.7 jit_solution(7056746250072353504)
XLA Ops:
  8.1 3.0 collective-permute-start.1
  11.2 6.3 collective-permute-done.1.refs_2_
  19.7 6.6 first.2
  26.3 6.0 all-to-all-start
  33.1 37.6 %all-gather.3.cloned.1.call-done.refs_3_.refs_4_.refs_5_.refs_2_ = bf16[32,256,256]{2,1,0:T(8,128)(2,1)} async-done(((bf16[32,64,256]{2,1,0:T(8,128)(2,1)}), bf16[32,256,256]{2,1,0:T(8,128)(2,1)}) %all-gather.3.cloned.1.call-update) | async-done | bytes 4194320 | tf_op jit(solution)/shard_map/all_gather | solution.py:402
  70.7 14.7 %first.3 = (bf16[8,3,16,8,1024]{4,3,2,1,0:T(8,128)(2,1)}, bf16[8,3,16,8,1024]{4,3,2,1,0:T(8,128)(2,1)}) custom-call(bf16[1024,8192]{1,0:T(8,128)(2,1)} %refs_2_.8, bf16[1024,8192]{1,0:T(8,128)(2,1)} %refs_2_.8, bf16[1024,8192]{1,0:T(8,128)(2,1)} %refs_2_.8, bf16[32,256,256]{2,1,0:T(8,128)(2,1)} %all-gather.3.cloned.1.call-done.refs_3_.refs_4_.refs_5_.refs_2_, ...), custom_call_target="tpu_custom_call" | custom-call | flops 3221225472 | bytes 28311552 | tf_op jit(solution)/shard_map/first/pallas_call | solution.py:110
  85.5 40.5 %all-to-all-done.refs_0_ = bf16[8,1,32,8,1024]{4,3,2,1,0:T(8,128)(2,1)} async-done(((bf16[8,1,32,8,1024]{4,3,2,1,0:T(8,128)(2,1)}), bf16[8,1,32,8,1024]{4,3,2,1,0:T(8,128)(2,1)}, u32[]{:S(2)}, u32[]{:S(2)}) %all-to-all-start) | async-done | bytes 4194336 | tf_op jit(solution)/shard_map/all_to_all | solution.py:351
  125.9 143.2 %all_to_all.30.refs_1_ = bf16[8,3,16,8,1024]{4,3,2,1,0:T(8,128)(2,1)} all-to-all(bf16[8,3,16,8,1024]{4,3,2,1,0:T(8,128)(2,1)} %get-tuple-element.39), channel_id=1, replica_groups=mesh['dp'=4,'mp'=8] {'mp'}, dimensions={0} | all-to-all | bytes 12582912 | tf_op jit(solution)/shard_map/all_to_all | solution.py:351
  269.2 4.8 all-to-all-start.2
  274.7 37.5 %all-gather.5.cloned.1.call-done.refs_2_ = bf16[32,256,256]{2,1,0:T(8,128)(2,1)} async-done(((bf16[32,64,256]{2,1,0:T(8,128)(2,1)}), bf16[32,256,256]{2,1,0:T(8,128)(2,1)}) %all-gather.5.cloned.1.call-update) | async-done | bytes 4194320 | tf_op jit(solution)/shard_map/all_gather | solution.py:403
  312.2 29.6 %middle.2 = (bf16[1024,8192]{1,0:T(8,128)(2,1)}, bf16[16,256,256]{2,1,0:T(8,128)(2,1)}, bf16[8,4,16,8,1024]{4,3,2,1,0:T(8,128)(2,1)}) custom-call(bf16[8,1,32,8,1024]{4,3,2,1,0:T(8,128)(2,1)} %all-to-all-done.refs_0_, bf16[8,3,16,8,1024]{4,3,2,1,0:T(8,128)(2,1)} %all_to_all.30.refs_1_, bf16[32,256,256]{2,1,0:T(8,128)(2,1)} %all-gather.5.cloned.1.call-done.refs_2_, ...), custom_call_target="tpu_custom_call" | custom-call | flops 6442450944 | bytes 46137344 | tf_op jit(solution)/shard_map/middle/pallas_call | solution.py:199
  341.8 69.2 %all-to-all-done.2.refs_1_ = bf16[8,3,16,8,1024]{4,3,2,1,0:T(8,128)(2,1)} async-done(((bf16[8,3,16,8,1024]{4,3,2,1,0:T(8,128)(2,1)}), bf16[8,3,16,8,1024]{4,3,2,1,0:T(8,128)(2,1)}, u32[]{:S(2)}, u32[]{:S(2)}) %all-to-all-start.2) | async-done | bytes 6291488 | tf_op jit(solution)/shard_map/all_to_all | solution.py:351
  411.0 5.0 all-to-all-start.3
  416.0 29.8 %middle.3 = (bf16[1024,8192]{1,0:T(8,128)(2,1)}, bf16[16,256,256]{2,1,0:T(8,128)(2,1)}, bf16[8,3,16,8,1024]{4,3,2,1,0:T(8,128)(2,1)}, bf16[8,1,16,8,1024]{4,3,2,1,0:T(8,128)(2,1)}) custom-call(bf16[8,1,32,8,1024]{4,3,2,1,0:T(8,128)(2,1)} %all-to-all-done.refs_0_, ...), custom_call_target="tpu_custom_call", output_to_operand_aliasing={{0}: (5, {})} | custom-call | flops 6442450944 | bytes 46137344 | tf_op jit(solution)/shard_map/middle/pallas_call | solution.py:199
  445.8 152.1 %all-to-all-done.3.refs_0_ = bf16[8,4,16,8,1024]{4,3,2,1,0:T(8,128)(2,1)} async-done(((bf16[8,4,16,8,1024]{4,3,2,1,0:T(8,128)(2,1)}), bf16[8,4,16,8,1024]{4,3,2,1,0:T(8,128)(2,1)}, u32[]{:S(2)}, u32[]{:S(2)}) %all-to-all-start.3) | async-done | bytes 8388640 | tf_op jit(solution)/shard_map/all_to_all | solution.py:351
  598.0 4.8 all-to-all-start.4
  604.1 35.4 %reduce-scatter.3.cloned.1.call-done = bf16[16,64,256]{2,1,0:T(8,128)(2,1)} async-done(((bf16[16,256,256]{2,1,0:T(8,128)(2,1)}), bf16[16,64,256]{2,1,0:T(8,128)(2,1)}) %reduce-scatter.3.cloned.1.call-update) | async-done | bytes 524304 | tf_op jit(solution)/shard_map/reduce_scatter | solution.py:388
  639.5 34.6 %reduce-scatter.5.cloned.1.call-done = bf16[16,64,256]{2,1,0:T(8,128)(2,1)} async-done(((bf16[16,256,256]{2,1,0:T(8,128)(2,1)}), bf16[16,64,256]{2,1,0:T(8,128)(2,1)}) %reduce-scatter.5.cloned.1.call-update) | async-done | bytes 524304 | tf_op jit(solution)/shard_map/reduce_scatter | solution.py:388
  674.1 66.1 %all-to-all-done.4.refs_1_ = bf16[8,3,16,8,1024]{4,3,2,1,0:T(8,128)(2,1)} async-done(((bf16[8,3,16,8,1024]{4,3,2,1,0:T(8,128)(2,1)}), bf16[8,3,16,8,1024]{4,3,2,1,0:T(8,128)(2,1)}, u32[]{:S(2)}, u32[]{:S(2)}) %all-to-all-start.4) | async-done | bytes 6291488 | tf_op jit(solution)/shard_map/all_to_all | solution.py:351
  740.2 3.8 all-to-all-start.5
  744.0 10.7 %last.5 = (bf16[2,8,64,256]{3,2,1,0:T(8,128)(2,1)}, bf16[2,8,64,256]{3,2,1,0:T(8,128)(2,1)}, bf16[1024,8192]{1,0:T(8,128)(2,1)}) custom-call(s32[1]{0:T(128)} %bitcast.position_ref, bf16[8,4,16,8,1024]{4,3,2,1,0:T(8,128)(2,1)} %all-to-all-done.3.refs_0_, bf16[8,3,16,8,1024]{4,3,2,1,0:T(8,128)(2,1)} %all-to-all-done.4.refs_1_, bf16[1024,8192]{1,0:T(8,128)(2,1)} %refs_2_.8, ...), custom_call_target="tpu_custom_call" | custom-call | flops 2147483648 | bytes 16777216 | tf_op jit(solution)/shard_map/last/pallas_call | solution.py:325
  754.7 10.7 %last.6 = (bf16[2,8,64,256]{3,2,1,0:T(8,128)(2,1)}, bf16[2,8,64,256]{3,2,1,0:T(8,128)(2,1)}, bf16[1024,8192]{1,0:T(8,128)(2,1)}) custom-call(s32[1]{0:T(128)} %bitcast.position_ref, bf16[8,4,16,8,1024]{4,3,2,1,0:T(8,128)(2,1)} %all-to-all-done.3.refs_0_, bf16[8,3,16,8,1024]{4,3,2,1,0:T(8,128)(2,1)} %all-to-all-done.4.refs_1_, ...), custom_call_target="tpu_custom_call", output_to_operand_aliasing={{2}: (6, {})} | custom-call | flops 2147483648 | bytes 16777216 | tf_op jit(solution)/shard_map/last/pallas_call | solution.py:325
  772.5 10.7 %last.7 = (bf16[2,8,64,256]{3,2,1,0:T(8,128)(2,1)}, bf16[2,8,64,256]{3,2,1,0:T(8,128)(2,1)}, bf16[1024,8192]{1,0:T(8,128)(2,1)}) custom-call(s32[1]{0:T(128)} %bitcast.position_ref, bf16[8,4,16,8,1024]{4,3,2,1,0:T(8,128)(2,1)} %all-to-all-done.3.refs_0_, bf16[8,3,16,8,1024]{4,3,2,1,0:T(8,128)(2,1)} %all-to-all-done.4.refs_1_, ...), custom_call_target="tpu_custom_call", output_to_operand_aliasing={{2}: (6, {})} | custom-call | flops 2147483648 | bytes 16777216 | tf_op jit(solution)/shard_map/last/pallas_call | solution.py:325
  783.2 2.0 collective-permute-done.5
  785.2 2.2 fusion.5
  787.3 5.0 all-to-all-done.5.refs_1_
  793.6 7.4 last.9
  804.4 1.6 collective-permute-start.8
  806.0 7.6 last.8
  813.6 2.6 maximum_convert_fusion
  816.2 2.2 collective-permute-done.8
  818.6 1.6 pad_maximum_fusion
  (51 shorter events, 17.8 us)
Async XLA Ops:
  8.1 10.9 %copy-start.3 = (bf16[8,64,256]{2,1,0:T(8,128)(2,1)}, bf16[8,64,256]{2,1,0:T(8,128)(2,1)S(1)}, u32[]{:S(2)}) copy-start(bf16[8,64,256]{2,1,0:T(8,128)(2,1)S(1)} %slice.17.refs_0_) | copy-start | bytes 786436
  8.1 9.3 %collective-permute-start.1 = (bf16[8,64,256]{2,1,0:T(8,128)(2,1)S(1)}, bf16[8,64,256]{2,1,0:T(8,128)(2,1)S(1)}, u32[]{:S(2)}, u32[]{:S(2)}) collective-permute-start(bf16[8,64,256]{2,1,0:T(8,128)(2,1)S(1)} %slice.17.refs_0_), channel_id=1, source_target_pairs={{0,16},{8,24},{16,0},{24,8},{1,17},{9,25},{17,1},{25,9},{2,18},{10... | collective-permute-start | bytes 786440 | tf_op jit(solution)/shard_map/ppermute | solution.py:360
  11.2 6.3 collective-permute-start
  17.5 1.5 copy-start.8
  17.5 1.5 collective-permute-start.2
  17.5 1.5 copy-start.9
  19.0 0.7 copy-start.10
  26.3 99.6 %all-to-all-start = ((bf16[8,1,32,8,1024]{4,3,2,1,0:T(8,128)(2,1)}), bf16[8,1,32,8,1024]{4,3,2,1,0:T(8,128)(2,1)}, u32[]{:S(2)}, u32[]{:S(2)}) async-start(bf16[8,1,32,8,1024]{4,3,2,1,0:T(8,128)(2,1)} %first.2), calls=%async_computation | async-start | bytes 8388608 | tf_op jit(solution)/shard_map/all_to_all | solution.py:351
  32.4 38.3 %all-gather.3.cloned.1.call-start = ((), (), s32[]{:S(2)}) async-start(), calls=%async_computation.8 | async-start | bytes 5242880 | tf_op jit(solution)/shard_map/all_gather | solution.py:402
  269.2 141.9 %all-to-all-start.2 = ((bf16[8,3,16,8,1024]{4,3,2,1,0:T(8,128)(2,1)}), bf16[8,3,16,8,1024]{4,3,2,1,0:T(8,128)(2,1)}, u32[]{:S(2)}, u32[]{:S(2)}) async-start(bf16[8,3,16,8,1024]{4,3,2,1,0:T(8,128)(2,1)} %get-tuple-element.40), calls=%async_computation.2 | async-start | bytes 12582912 | tf_op jit(solution)/shard_map/all_to_all | solution.py:351
  273.9 38.3 %all-gather.5.cloned.1.call-start = ((), (), s32[]{:S(2)}) async-start(), calls=%async_computation.9 | async-start | bytes 5242880 | tf_op jit(solution)/shard_map/all_gather | solution.py:403
  411.0 187.0 %all-to-all-start.3 = ((bf16[8,4,16,8,1024]{4,3,2,1,0:T(8,128)(2,1)}), bf16[8,4,16,8,1024]{4,3,2,1,0:T(8,128)(2,1)}, u32[]{:S(2)}, u32[]{:S(2)}) async-start(bf16[8,4,16,8,1024]{4,3,2,1,0:T(8,128)(2,1)} %get-tuple-element.45), calls=%async_computation.3 | async-start | bytes 16777216 | tf_op jit(solution)/shard_map/all_to_all | solution.py:351
  598.0 142.2 %all-to-all-start.4 = ((bf16[8,3,16,8,1024]{4,3,2,1,0:T(8,128)(2,1)}), bf16[8,3,16,8,1024]{4,3,2,1,0:T(8,128)(2,1)}, u32[]{:S(2)}, u32[]{:S(2)}) async-start(bf16[8,3,16,8,1024]{4,3,2,1,0:T(8,128)(2,1)} %get-tuple-element.48), calls=%async_computation.4 | async-start | bytes 12582912 | tf_op jit(solution)/shard_map/all_to_all | solution.py:351
  602.8 36.7 %reduce-scatter.3.cloned.1.call-start = ((), (), s32[]{:S(2)}) async-start(), calls=%async_computation.10 | async-start | bytes 2621440 | tf_op jit(solution)/shard_map/reduce_scatter | solution.py:388
  603.5 70.6 %reduce-scatter.5.cloned.1.call-start = ((), (), s32[]{:S(2)}) async-start(), calls=%async_computation.11 | async-start | bytes 2621440 | tf_op jit(solution)/shard_map/reduce_scatter | solution.py:388
  740.2 52.1 %all-to-all-start.5 = ((bf16[8,1,16,8,1024]{4,3,2,1,0:T(8,128)(2,1)}), bf16[8,1,16,8,1024]{4,3,2,1,0:T(8,128)(2,1)S(1)}, u32[]{:S(2)}, u32[]{:S(2)}) async-start(bf16[8,1,16,8,1024]{4,3,2,1,0:T(8,128)(2,1)} %get-tuple-element.51), calls=%async_computation.7 | async-start | bytes 4194304 | tf_op jit(solution)/shard_map/all_to_all | solution.py:351
  754.7 11.3 %collective-permute-start.3 = (bf16[2,8,64,256]{3,2,1,0:T(8,128)(2,1)}, bf16[2,8,64,256]{3,2,1,0:T(8,128)(2,1)S(1)}, u32[]{:S(2)}, u32[]{:S(2)}) collective-permute-start(bf16[2,8,64,256]{3,2,1,0:T(8,128)(2,1)} %get-tuple-element.53), channel_id=1, source_target_pairs={{0,8},{8,0},{16,24},{24,16},{1,9},{9,1},{17,25},{25,17},{2,10},{10... | collective-permute-start | bytes 1572872 | tf_op jit(solution)/shard_map/ppermute | solution.py:360
  754.7 12.1 %copy-start.6 = (bf16[2,8,64,256]{3,2,1,0:T(8,128)(2,1)S(1)}, bf16[2,8,64,256]{3,2,1,0:T(8,128)(2,1)}, u32[]{:S(2)}) copy-start(bf16[2,8,64,256]{3,2,1,0:T(8,128)(2,1)} %get-tuple-element.52) | copy-start | bytes 1572868
  765.5 2.5 collective-permute-start.4
  766.0 0.8 copy-start.7
  769.2 1.0 copy-start.1
  771.0 14.2 %collective-permute-start.5 = (bf16[1,16,64,256]{3,2,1,0:T(8,128)(2,1)}, bf16[1,16,64,256]{3,2,1,0:T(8,128)(2,1)S(1)}, u32[]{:S(2)}, u32[]{:S(2)}) collective-permute-start(bf16[1,16,64,256]{3,2,1,0:T(8,128)(2,1)} %fusion.7), channel_id=1, source_target_pairs={{0,16},{8,24},{16,0},{24,8},{1,17},{9,25},{17,1},{25,9},{2,18},{10... | collective-permute-start | bytes 1572872 | tf_op jit(solution)/shard_map/ppermute | solution.py:360
  783.2 17.9 %collective-permute-start.6 = (bf16[2,8,64,256]{3,2,1,0:T(8,128)(2,1)}, bf16[2,8,64,256]{3,2,1,0:T(8,128)(2,1)}, u32[]{:S(2)}, u32[]{:S(2)}) collective-permute-start(bf16[2,8,64,256]{3,2,1,0:T(8,128)(2,1)} %get-tuple-element.61), channel_id=1, source_target_pairs={{0,8},{8,0},{16,24},{24,16},{1,9},{9,1},{17,25},{25,17},{2,10},{10... | collective-permute-start | bytes 1572872 | tf_op jit(solution)/shard_map/ppermute | solution.py:360
  787.3 13.7 %copy-start.5 = (bf16[2,8,64,256]{3,2,1,0:T(8,128)(2,1)S(1)}, bf16[2,8,64,256]{3,2,1,0:T(8,128)(2,1)}, u32[]{:S(2)}) copy-start(bf16[2,8,64,256]{3,2,1,0:T(8,128)(2,1)} %get-tuple-element.60) | copy-start | bytes 1572868
  792.3 1.3 copy-start
  801.0 2.1 collective-permute-start.7
  804.4 14.0 %collective-permute-start.8 = (bf16[1,16,64,256]{3,2,1,0:T(8,128)(2,1)S(1)}, bf16[1,16,64,256]{3,2,1,0:T(8,128)(2,1)S(1)}, u32[]{:S(2)}, u32[]{:S(2)}) collective-permute-start(bf16[1,16,64,256]{3,2,1,0:T(8,128)(2,1)S(1)} %fusion.6), channel_id=1, source_target_pairs={{0,16},{8,24},{16,0},{24,8},{1,17},{9,25},{17,1},{25,9},{2,18},{10... | collective-permute-start | bytes 1572872 | tf_op jit(solution)/shard_map/ppermute | solution.py:360
  806.0 7.6 copy-start.4
  813.6 5.0 copy-start.2
Sparse Core Ops, SparseCore 0:
  34.8 35.9 all-gather.2
  276.3 35.8 all-gather.4
  606.7 32.7 reduce-scatter.2
  642.6 31.4 reduce-scatter.4
where the time goes:
time: 828 us; the launch traced here: 827 us
  waiting for transfers between devices  494 us (60%)
  blocking collectives  143 us (17%)
  Pallas kernels  128 us (15%)
  starting transfers between devices  31.2 us (4%)
  between operations  13.9 us (2%)
  other arithmetic  12 us (1%)
    all_to_all x5, waiting for transfers between devices, exchange(): return lax.all_to_all(array, 'mp', split_axis=0, concat_axis=0, tiled=True)  333 us
    all_to_all x1, blocking collectives, exchange(): return lax.all_to_all(array, 'mp', split_axis=0, concat_axis=0, tiled=True)  143 us
    reduce_scatter x2, waiting for transfers between devices, scatter(): return lax.psum_scatter(part, 'dp', scatter_dimension=1, tiled=True)  70 us
    pallas_call x2, Pallas kernels, middle_part(): pl.pallas_call(functools.partial(middle_kernel, owners, group, sources, b...  59.4 us
    pallas_call x5, Pallas kernels, last_part(): pl.pallas_call(functools.partial(last_kernel, held, sources, shares, rows...  47.2 us
    all_gather x1, waiting for transfers between devices, on_device(): w_one = lax.all_gather(after(factor_one, head), 'dp', axis=1, tiled=True)  37.6 us
    all_gather x1, waiting for transfers between devices, on_device(): w_two = lax.all_gather(after(factor_two, w_one), 'dp', axis=1, tiled=True)  37.5 us
    all_to_all x5, starting transfers between devices, exchange(): return lax.all_to_all(array, 'mp', split_axis=0, concat_axis=0, tiled=True)  24.3 us
  transfers between devices with their start and end apart: 18, of which 14 were waited for; matrix products, arithmetic and copies ran while one was open for 1% of the time, Pallas kernels for 15%

commit v1 on v0

--- a/solution.py
+++ b/solution.py
@@ -25,17 +25,18 @@
     for b in range(group):
         rows = contract(weight[b], feat_ref[:, b * width : (b + 1) * width], 1, 1)
         for lane in range(tokens // LANES):
-            swap[lane, pl.ds(b, width, stride=group), :] = rows[
+            swap[lane, pl.ds(b, width, stride=group + 1), :] = rows[
                 :, lane * LANES : (lane + 1) * LANES
             ]
     for out_ref, (low, high) in zip(out_refs, cuts):
         for owner in range(owners):
-            start = (owner * held + low) * group
-            for lane in range(tokens // LANES):
-                block = swap[lane, pl.ds(start, (high - low) * group), :]
-                out_ref[owner, unit, :, :, lane * LANES : (lane + 1) * LANES] = block.reshape(
-                    high - low, group, LANES
-                ).astype(jnp.bfloat16)
+            for j in range(low, high):
+                start = (owner * held + j) * (group + 1)
+                for lane in range(tokens // LANES):
+                    block = swap[lane, pl.ds(start, group), :]
+                    out_ref[owner, unit, j - low, :, lane * LANES : (lane + 1) * LANES] = (
+                        block.astype(jnp.bfloat16)
+                    )
 
 
 def first_kernel(cuts, owners, held, units, *refs):
@@ -84,7 +85,7 @@
         pl.BlockSpec((owners, units, high - low, group, tile), lambda t, *_: (0, 0, 0, 0, t))
         for low, high in cuts
     ]
-    swap = pltpu.VMEM((tile // LANES, width * group, LANES), jnp.float32)
+    swap = pltpu.VMEM((tile // LANES, width * (group + 1), LANES), jnp.float32)
     params = dict(
         out_shape=outs,
         compiler_params=pltpu.CompilerParams(vmem_limit_bytes=VMEM_LIMIT),
@@ -233,7 +234,7 @@
     swap = refs.pop(0)
     total = refs.pop(0) if rows_out else None
     group, tokens = q_refs[0].shape[3:]
-    width = swap.shape[1] // group
+    width = swap.shape[1] // (group + 1)
     lanes = tokens // LANES
     step = pl.program_id(0)
 
@@ -245,15 +246,14 @@
 
     for q_ref, (low, high) in zip(q_refs, sources):
         for owner in range(q_ref.shape[0]):
-            start = (owner * held + low) * group
-            for lane in range(lanes):
-                block = q_ref[owner, 0, :, :, lane * LANES : (lane + 1) * LANES]
-                swap[lane, pl.ds(start, (high - low) * group), :] = block.astype(
-                    jnp.float32
-                ).reshape((high - low) * group, LANES)
+            for j in range(low, high):
+                start = (owner * held + j) * (group + 1)
+                for lane in range(lanes):
+                    block = q_ref[owner, 0, j - low, :, lane * LANES : (lane + 1) * LANES]
+                    swap[lane, pl.ds(start, group), :] = block.astype(jnp.float32)
     for b in range(group):
         back = jnp.concatenate(
-            [swap[lane, pl.ds(b, width, stride=group), :] for lane in range(lanes)], axis=1
+            [swap[lane, pl.ds(b, width, stride=group + 1), :] for lane in range(lanes)], axis=1
         ).astype(jnp.bfloat16)
         columns = slice(b * width, (b + 1) * width)
         if grad_out:
@@ -302,7 +302,7 @@
         sources.append((low, low + count))
         low += count
     outs, out_specs, aliases = [], [], {}
-    scratch = [pltpu.VMEM((tile // LANES, width * group, LANES), jnp.float32)]
+    scratch = [pltpu.VMEM((tile // LANES, width * (group + 1), LANES), jnp.float32)]
     chained = 1 if grad_of is not None and grad is not None else 0
     if rows_of is not None:
         operands.append(rows_of)
@@ -420,9 +420,11 @@
     layer, part_high, *back_high = middle_part(
         received[1], w_two, features, cotangent, layer, half, held, backs
     )
-    parts_two = [scatter(part_low), scatter(part_high)]
+    grad_two = jnp.concatenate([scatter(part_low), scatter(part_high)], axis=0).astype(
+        jnp.float32
+    )
     for index, array in enumerate(back_high):
-        before = (latest, parts_two) if index else latest
+        before = (latest, grad_two) if index else latest
         latest = back_high[index] = exchange(array, before)
 
     grad, hops, parts_one = None, [], []
@@ -441,9 +443,10 @@
                 position, returned, index, features, grad_of, grad, shares
             )
         hops.append(first_hop(keep, send))
-        if index == units // 2 - 1 or index == units - 1:
-            parts_one.append(other_hops(hops[-(units // 2 or 1) :]))
-    parts_two = after(parts_two, hops[-1])
+        if index == units - 3:
+            parts_one.append(other_hops(hops))
+        elif index >= units - 2:
+            parts_one.append(other_hops(hops[-1:]))
     grad_one = jnp.concatenate(parts_one[:-1] + [jnp.zeros_like(parts_one[-1])], axis=0)
     start = held - parts_one[-1].shape[0]
     grad_one = lax.dynamic_update_slice(grad_one, parts_one[-1], (start, 0, 0))
@@ -451,7 +454,7 @@
         layer,
         grad,
         grad_one,
-        jnp.concatenate(parts_two, axis=0).astype(jnp.float32),
+        grad_two,
     )
 
 

time: 828 us -> 829 us (level)
    ppermute x9 -> x10, waiting for transfers between devices: 13 us -> 27.4 us  [swap_with(): return lax.ppermute(array, 'dp', [(d, d ^ step) for d in range(size)])]
  transfers between devices with their start and end apart: 18 -> 19, of which waited for: 14 -> 12; matrix products, arithmetic and copies ran while one was open for 1% -> 1% of each run, Pallas kernels for 15% -> 13%
where the time goes in v1:
time: 829 us; the launch traced here: 828 us
  waiting for transfers between devices  502 us (61%)
  blocking collectives  143 us (17%)
  Pallas kernels  124 us (15%)
  starting transfers between devices  32 us (4%)
  between operations  13.9 us (2%)
  other arithmetic  9.75 us (1%)
    all_to_all x5, waiting for transfers between devices, exchange(): return lax.all_to_all(array, 'mp', split_axis=0, concat_axis=0, tiled=True)  326 us
    all_to_all x1, blocking collectives, exchange(): return lax.all_to_all(array, 'mp', split_axis=0, concat_axis=0, tiled=True)  143 us
    reduce_scatter x2, waiting for transfers between devices, scatter(): return lax.psum_scatter(part, 'dp', scatter_dimension=1, tiled=True)  70 us
    pallas_call x2, Pallas kernels, middle_part(): pl.pallas_call(functools.partial(middle_kernel, owners, group, sources, b...  59.4 us
    pallas_call x5, Pallas kernels, last_part(): pl.pallas_call(functools.partial(last_kernel, held, sources, shares, rows...  44.7 us
    all_gather x1, waiting for transfers between devices, on_device(): w_one = lax.all_gather(after(factor_one, head), 'dp', axis=1, tiled=True)  37.6 us
    all_gather x1, waiting for transfers between devices, on_device(): w_two = lax.all_gather(after(factor_two, w_one), 'dp', axis=1, tiled=True)  37.5 us
    ppermute x10, waiting for transfers between devices, swap_with(): return lax.ppermute(array, 'dp', [(d, d ^ step) for d in range(size)])  27.4 us
  transfers between devices with their start and end apart: 19, of which 12 were waited for; matrix products, arithmetic and copies ran while one was open for 1% of the time, Pallas kernels for 13%

profile of v1, /device:TPU:0, one launch (start us, length us, event | category | flops | bytes accessed | tf_op | source)
XLA Modules:
  0.0 827.9 jit_solution(12158121781633449926)
XLA Ops:
  8.1 3.0 collective-permute-start.1
  11.2 6.3 collective-permute-done.1.refs_2_
  17.5 1.5 collective-permute-done.2.refs_3_
  19.7 6.5 first.2
  26.2 6.0 all-to-all-start
  32.9 37.6 %all-gather.3.cloned.1.call-done.refs_3_.refs_4_.refs_5_.refs_2_ = bf16[32,256,256]{2,1,0:T(8,128)(2,1)} async-done(((bf16[32,64,256]{2,1,0:T(8,128)(2,1)}), bf16[32,256,256]{2,1,0:T(8,128)(2,1)}) %all-gather.3.cloned.1.call-update) | async-done | bytes 4194320 | tf_op jit(solution)/shard_map/all_gather | solution.py:402
  70.6 13.7 %first.3 = (bf16[8,3,16,8,1024]{4,3,2,1,0:T(8,128)(2,1)}, bf16[8,3,16,8,1024]{4,3,2,1,0:T(8,128)(2,1)}) custom-call(bf16[1024,8192]{1,0:T(8,128)(2,1)} %refs_2_.8, bf16[1024,8192]{1,0:T(8,128)(2,1)} %refs_2_.8, bf16[1024,8192]{1,0:T(8,128)(2,1)} %refs_2_.8, bf16[32,256,256]{2,1,0:T(8,128)(2,1)} %all-gather.3.cloned.1.call-done.refs_3_.refs_4_.refs_5_.refs_2_, ...), custom_call_target="tpu_custom_call" | custom-call | flops 3221225472 | bytes 28311552 | tf_op jit(solution)/shard_map/first/pallas_call | solution.py:111
  84.3 41.6 %all-to-all-done.refs_0_ = bf16[8,1,32,8,1024]{4,3,2,1,0:T(8,128)(2,1)} async-done(((bf16[8,1,32,8,1024]{4,3,2,1,0:T(8,128)(2,1)}), bf16[8,1,32,8,1024]{4,3,2,1,0:T(8,128)(2,1)}, u32[]{:S(2)}, u32[]{:S(2)}) %all-to-all-start) | async-done | bytes 4194336 | tf_op jit(solution)/shard_map/all_to_all | solution.py:351
  125.8 143.3 %all_to_all.30.refs_1_ = bf16[8,3,16,8,1024]{4,3,2,1,0:T(8,128)(2,1)} all-to-all(bf16[8,3,16,8,1024]{4,3,2,1,0:T(8,128)(2,1)} %get-tuple-element.37), channel_id=1, replica_groups=mesh['dp'=4,'mp'=8] {'mp'}, dimensions={0} | all-to-all | bytes 12582912 | tf_op jit(solution)/shard_map/all_to_all | solution.py:351
  269.1 4.8 all-to-all-start.2
  274.6 37.5 %all-gather.5.cloned.1.call-done.refs_2_ = bf16[32,256,256]{2,1,0:T(8,128)(2,1)} async-done(((bf16[32,64,256]{2,1,0:T(8,128)(2,1)}), bf16[32,256,256]{2,1,0:T(8,128)(2,1)}) %all-gather.5.cloned.1.call-update) | async-done | bytes 4194320 | tf_op jit(solution)/shard_map/all_gather | solution.py:403
  312.2 29.6 %middle.2 = (bf16[1024,8192]{1,0:T(8,128)(2,1)}, bf16[16,256,256]{2,1,0:T(8,128)(2,1)}, bf16[8,4,16,8,1024]{4,3,2,1,0:T(8,128)(2,1)}) custom-call(bf16[8,1,32,8,1024]{4,3,2,1,0:T(8,128)(2,1)} %all-to-all-done.refs_0_, bf16[8,3,16,8,1024]{4,3,2,1,0:T(8,128)(2,1)} %all_to_all.30.refs_1_, bf16[32,256,256]{2,1,0:T(8,128)(2,1)} %all-gather.5.cloned.1.call-done.refs_2_, ...), custom_call_target="tpu_custom_call" | custom-call | flops 6442450944 | bytes 46137344 | tf_op jit(solution)/shard_map/middle/pallas_call | solution.py:200
  341.7 69.3 %all-to-all-done.2.refs_1_ = bf16[8,3,16,8,1024]{4,3,2,1,0:T(8,128)(2,1)} async-done(((bf16[8,3,16,8,1024]{4,3,2,1,0:T(8,128)(2,1)}), bf16[8,3,16,8,1024]{4,3,2,1,0:T(8,128)(2,1)}, u32[]{:S(2)}, u32[]{:S(2)}) %all-to-all-start.2) | async-done | bytes 6291488 | tf_op jit(solution)/shard_map/all_to_all | solution.py:351
  411.0 5.0 all-to-all-start.3
  416.0 29.8 %middle.3 = (bf16[1024,8192]{1,0:T(8,128)(2,1)}, bf16[16,256,256]{2,1,0:T(8,128)(2,1)}, bf16[8,3,16,8,1024]{4,3,2,1,0:T(8,128)(2,1)}, bf16[8,1,16,8,1024]{4,3,2,1,0:T(8,128)(2,1)}) custom-call(bf16[8,1,32,8,1024]{4,3,2,1,0:T(8,128)(2,1)} %all-to-all-done.refs_0_, ...), custom_call_target="tpu_custom_call", output_to_operand_aliasing={{0}: (5, {})} | custom-call | flops 6442450944 | bytes 46137344 | tf_op jit(solution)/shard_map/middle/pallas_call | solution.py:200
  445.8 152.2 %all-to-all-done.3.refs_0_ = bf16[8,4,16,8,1024]{4,3,2,1,0:T(8,128)(2,1)} async-done(((bf16[8,4,16,8,1024]{4,3,2,1,0:T(8,128)(2,1)}), bf16[8,4,16,8,1024]{4,3,2,1,0:T(8,128)(2,1)}, u32[]{:S(2)}, u32[]{:S(2)}) %all-to-all-start.3) | async-done | bytes 8388640 | tf_op jit(solution)/shard_map/all_to_all | solution.py:351
  598.0 4.8 all-to-all-start.4
  604.1 35.4 %reduce-scatter.3.cloned.1.call-done = bf16[16,64,256]{2,1,0:T(8,128)(2,1)} async-done(((bf16[16,256,256]{2,1,0:T(8,128)(2,1)}), bf16[16,64,256]{2,1,0:T(8,128)(2,1)}) %reduce-scatter.3.cloned.1.call-update) | async-done | bytes 524304 | tf_op jit(solution)/shard_map/reduce_scatter | solution.py:388
  639.5 34.6 %reduce-scatter.5.cloned.1.call-done = bf16[16,64,256]{2,1,0:T(8,128)(2,1)} async-done(((bf16[16,256,256]{2,1,0:T(8,128)(2,1)}), bf16[16,64,256]{2,1,0:T(8,128)(2,1)}) %reduce-scatter.5.cloned.1.call-update) | async-done | bytes 524304 | tf_op jit(solution)/shard_map/reduce_scatter | solution.py:388
  674.1 2.7 maximum_convert_fusion
  676.7 63.4 %all-to-all-done.4.refs_1_ = bf16[8,3,16,8,1024]{4,3,2,1,0:T(8,128)(2,1)} async-done(((bf16[8,3,16,8,1024]{4,3,2,1,0:T(8,128)(2,1)}), bf16[8,3,16,8,1024]{4,3,2,1,0:T(8,128)(2,1)}, u32[]{:S(2)}, u32[]{:S(2)}) %all-to-all-start.4) | async-done | bytes 6291488 | tf_op jit(solution)/shard_map/all_to_all | solution.py:351
  740.1 3.8 all-to-all-start.5
  743.9 10.1 %last.5 = (bf16[2,8,64,256]{3,2,1,0:T(8,128)(2,1)}, bf16[2,8,64,256]{3,2,1,0:T(8,128)(2,1)}, bf16[1024,8192]{1,0:T(8,128)(2,1)}) custom-call(s32[1]{0:T(128)} %bitcast.position_ref, bf16[8,4,16,8,1024]{4,3,2,1,0:T(8,128)(2,1)} %all-to-all-done.3.refs_0_, bf16[8,3,16,8,1024]{4,3,2,1,0:T(8,128)(2,1)} %all-to-all-done.4.refs_1_, bf16[1024,8192]{1,0:T(8,128)(2,1)} %refs_2_.8, ...), custom_call_target="tpu_custom_call" | custom-call | flops 2147483648 | bytes 16777216 | tf_op jit(solution)/shard_map/last/pallas_call | solution.py:325
  754.1 10.1 %last.6 = (bf16[2,8,64,256]{3,2,1,0:T(8,128)(2,1)}, bf16[2,8,64,256]{3,2,1,0:T(8,128)(2,1)}, bf16[1024,8192]{1,0:T(8,128)(2,1)}) custom-call(s32[1]{0:T(128)} %bitcast.position_ref, bf16[8,4,16,8,1024]{4,3,2,1,0:T(8,128)(2,1)} %all-to-all-done.3.refs_0_, bf16[8,3,16,8,1024]{4,3,2,1,0:T(8,128)(2,1)} %all-to-all-done.4.refs_1_, ...), custom_call_target="tpu_custom_call", output_to_operand_aliasing={{2}: (6, {})} | custom-call | flops 2147483648 | bytes 16777216 | tf_op jit(solution)/shard_map/last/pallas_call | solution.py:325
  764.7 10.2 %last.7 = (bf16[2,8,64,256]{3,2,1,0:T(8,128)(2,1)}, bf16[2,8,64,256]{3,2,1,0:T(8,128)(2,1)}, bf16[1024,8192]{1,0:T(8,128)(2,1)}) custom-call(s32[1]{0:T(128)} %bitcast.position_ref, bf16[8,4,16,8,1024]{4,3,2,1,0:T(8,128)(2,1)} %all-to-all-done.3.refs_0_, bf16[8,3,16,8,1024]{4,3,2,1,0:T(8,128)(2,1)} %all-to-all-done.4.refs_1_, ...), custom_call_target="tpu_custom_call", output_to_operand_aliasing={{2}: (6, {})} | custom-call | flops 2147483648 | bytes 16777216 | tf_op jit(solution)/shard_map/last/pallas_call | solution.py:325
  776.3 1.6 collective-permute-start.5
  778.8 17.5 %collective-permute-done.7 = bf16[1,8,64,256]{3,2,1,0:T(8,128)(2,1)S(1)} collective-permute-done((bf16[1,8,64,256]{3,2,1,0:T(8,128)(2,1)S(1)}, bf16[1,8,64,256]{3,2,1,0:T(8,128)(2,1)S(1)}, u32[]{:S(2)}, u32[]{:S(2)}) %collective-permute-start.7) | collective-permute-done | bytes 262176 | tf_op jit(solution)/shard_map/ppermute | solution.py:360
  798.7 7.1 last.9
  805.9 2.0 collective-permute-done.8
  809.2 1.6 collective-permute-start.9
  810.8 2.6 maximum_maximum_fusion
  813.3 7.2 last.8
  (51 shorter events, 11.7 us)
Async XLA Ops:
  8.1 10.9 %copy-start.1 = (bf16[8,64,256]{2,1,0:T(8,128)(2,1)}, bf16[8,64,256]{2,1,0:T(8,128)(2,1)S(1)}, u32[]{:S(2)}) copy-start(bf16[8,64,256]{2,1,0:T(8,128)(2,1)S(1)} %slice.24.refs_0_) | copy-start | bytes 786436
  8.1 9.3 %collective-permute-start.1 = (bf16[8,64,256]{2,1,0:T(8,128)(2,1)S(1)}, bf16[8,64,256]{2,1,0:T(8,128)(2,1)S(1)}, u32[]{:S(2)}, u32[]{:S(2)}) collective-permute-start(bf16[8,64,256]{2,1,0:T(8,128)(2,1)S(1)} %slice.24.refs_0_), channel_id=1, source_target_pairs={{0,16},{8,24},{16,0},{24,8},{1,17},{9,25},{17,1},{25,9},{2,18},{10... | collective-permute-start | bytes 786440 | tf_op jit(solution)/shard_map/ppermute | solution.py:360
  11.2 6.3 collective-permute-start
  17.5 1.5 copy-start.5
  17.5 1.5 collective-permute-start.2
  17.5 1.5 copy-start.6
  19.0 0.7 copy-start.7
  26.2 99.6 %all-to-all-start = ((bf16[8,1,32,8,1024]{4,3,2,1,0:T(8,128)(2,1)}), bf16[8,1,32,8,1024]{4,3,2,1,0:T(8,128)(2,1)}, u32[]{:S(2)}, u32[]{:S(2)}) async-start(bf16[8,1,32,8,1024]{4,3,2,1,0:T(8,128)(2,1)} %first.2), calls=%async_computation | async-start | bytes 8388608 | tf_op jit(solution)/shard_map/all_to_all | solution.py:351
  32.2 38.3 %all-gather.3.cloned.1.call-start = ((), (), s32[]{:S(2)}) async-start(), calls=%async_computation.8 | async-start | bytes 5242880 | tf_op jit(solution)/shard_map/all_gather | solution.py:402
  269.1 141.9 %all-to-all-start.2 = ((bf16[8,3,16,8,1024]{4,3,2,1,0:T(8,128)(2,1)}), bf16[8,3,16,8,1024]{4,3,2,1,0:T(8,128)(2,1)}, u32[]{:S(2)}, u32[]{:S(2)}) async-start(bf16[8,3,16,8,1024]{4,3,2,1,0:T(8,128)(2,1)} %get-tuple-element.38), calls=%async_computation.2 | async-start | bytes 12582912 | tf_op jit(solution)/shard_map/all_to_all | solution.py:351
  273.9 38.3 %all-gather.5.cloned.1.call-start = ((), (), s32[]{:S(2)}) async-start(), calls=%async_computation.9 | async-start | bytes 5242880 | tf_op jit(solution)/shard_map/all_gather | solution.py:403
  411.0 187.0 %all-to-all-start.3 = ((bf16[8,4,16,8,1024]{4,3,2,1,0:T(8,128)(2,1)}), bf16[8,4,16,8,1024]{4,3,2,1,0:T(8,128)(2,1)}, u32[]{:S(2)}, u32[]{:S(2)}) async-start(bf16[8,4,16,8,1024]{4,3,2,1,0:T(8,128)(2,1)} %get-tuple-element.43), calls=%async_computation.3 | async-start | bytes 16777216 | tf_op jit(solution)/shard_map/all_to_all | solution.py:351
  598.0 142.2 %all-to-all-start.4 = ((bf16[8,3,16,8,1024]{4,3,2,1,0:T(8,128)(2,1)}), bf16[8,3,16,8,1024]{4,3,2,1,0:T(8,128)(2,1)}, u32[]{:S(2)}, u32[]{:S(2)}) async-start(bf16[8,3,16,8,1024]{4,3,2,1,0:T(8,128)(2,1)} %get-tuple-element.46), calls=%async_computation.4 | async-start | bytes 12582912 | tf_op jit(solution)/shard_map/all_to_all | solution.py:351
  602.8 36.7 %reduce-scatter.3.cloned.1.call-start = ((), (), s32[]{:S(2)}) async-start(), calls=%async_computation.10 | async-start | bytes 2621440 | tf_op jit(solution)/shard_map/reduce_scatter | solution.py:388
  603.5 70.6 %reduce-scatter.5.cloned.1.call-start = ((), (), s32[]{:S(2)}) async-start(), calls=%async_computation.11 | async-start | bytes 2621440 | tf_op jit(solution)/shard_map/reduce_scatter | solution.py:388
  740.1 57.2 %all-to-all-start.5 = ((bf16[8,1,16,8,1024]{4,3,2,1,0:T(8,128)(2,1)}), bf16[8,1,16,8,1024]{4,3,2,1,0:T(8,128)(2,1)S(1)}, u32[]{:S(2)}, u32[]{:S(2)}) async-start(bf16[8,1,16,8,1024]{4,3,2,1,0:T(8,128)(2,1)} %get-tuple-element.49), calls=%async_computation.7 | async-start | bytes 4194304 | tf_op jit(solution)/shard_map/all_to_all | solution.py:351
  754.1 20.9 %collective-permute-start.3 = (bf16[2,8,64,256]{3,2,1,0:T(8,128)(2,1)}, bf16[2,8,64,256]{3,2,1,0:T(8,128)(2,1)S(1)}, u32[]{:S(2)}, u32[]{:S(2)}) collective-permute-start(bf16[2,8,64,256]{3,2,1,0:T(8,128)(2,1)} %get-tuple-element.51), channel_id=1, source_target_pairs={{0,8},{8,0},{16,24},{24,16},{1,9},{9,1},{17,25},{25,17},{2,10},{10... | collective-permute-start | bytes 1572872 | tf_op jit(solution)/shard_map/ppermute | solution.py:360
  764.2 10.9 %collective-permute-start.4 = (bf16[2,8,64,256]{3,2,1,0:T(8,128)(2,1)}, bf16[2,8,64,256]{3,2,1,0:T(8,128)(2,1)}, u32[]{:S(2)}, u32[]{:S(2)}) collective-permute-start(bf16[2,8,64,256]{3,2,1,0:T(8,128)(2,1)} %get-tuple-element.54), channel_id=1, source_target_pairs={{0,8},{8,0},{16,24},{24,16},{1,9},{9,1},{17,25},{25,17},{2,10},{10... | collective-permute-start | bytes 1572872 | tf_op jit(solution)/shard_map/ppermute | solution.py:360
  764.7 10.3 %copy-start.3 = (bf16[2,8,64,256]{3,2,1,0:T(8,128)(2,1)S(1)}, bf16[2,8,64,256]{3,2,1,0:T(8,128)(2,1)}, u32[]{:S(2)}) copy-start(bf16[2,8,64,256]{3,2,1,0:T(8,128)(2,1)} %get-tuple-element.50) | copy-start | bytes 1572868
  764.7 10.4 %copy-start.4 = (bf16[2,8,64,256]{3,2,1,0:T(8,128)(2,1)S(1)}, bf16[2,8,64,256]{3,2,1,0:T(8,128)(2,1)}, u32[]{:S(2)}) copy-start(bf16[2,8,64,256]{3,2,1,0:T(8,128)(2,1)} %get-tuple-element.53) | copy-start | bytes 1572868
  774.9 3.1 copy-start.2
  774.9 3.1 collective-permute-start.6
  776.3 20.9 %collective-permute-start.5 = (bf16[1,16,64,256]{3,2,1,0:T(8,128)(2,1)S(1)}, bf16[1,16,64,256]{3,2,1,0:T(8,128)(2,1)S(1)}, u32[]{:S(2)}, u32[]{:S(2)}) collective-permute-start(bf16[1,16,64,256]{3,2,1,0:T(8,128)(2,1)S(1)} %fusion.3), channel_id=1, source_target_pairs={{0,16},{8,24},{16,0},{24,8},{1,17},{9,25},{17,1},{25,9},{2,18},{10... | collective-permute-start | bytes 1572872 | tf_op jit(solution)/shard_map/ppermute | solution.py:360
  778.1 18.2 %collective-permute-start.7 = (bf16[1,8,64,256]{3,2,1,0:T(8,128)(2,1)S(1)}, bf16[1,8,64,256]{3,2,1,0:T(8,128)(2,1)S(1)}, u32[]{:S(2)}, u32[]{:S(2)}) collective-permute-start(bf16[1,8,64,256]{3,2,1,0:T(8,128)(2,1)S(1)} %slice.58), channel_id=1, source_target_pairs={{0,16},{8,24},{16,0},{24,8},{1,17},{9,25},{17,1},{25,9},{2,18},{10... | collective-permute-start | bytes 786440 | tf_op jit(solution)/shard_map/ppermute | solution.py:360
  797.4 1.4 copy-start
  805.8 2.1 collective-permute-start.8
  809.2 11.3 %collective-permute-start.9 = (bf16[1,8,64,256]{3,2,1,0:T(8,128)(2,1)S(1)}, bf16[1,8,64,256]{3,2,1,0:T(8,128)(2,1)S(1)}, u32[]{:S(2)}, u32[]{:S(2)}) collective-permute-start(bf16[1,8,64,256]{3,2,1,0:T(8,128)(2,1)S(1)} %slice.57), channel_id=1, source_target_pairs={{0,16},{8,24},{16,0},{24,8},{1,17},{9,25},{17,1},{25,9},{2,18},{10... | collective-permute-start | bytes 786440 | tf_op jit(solution)/shard_map/ppermute | solution.py:360
Sparse Core Ops, SparseCore 0:
  34.6 35.8 all-gather.2
  276.3 35.8 all-gather.4
  606.7 32.7 reduce-scatter.2
  642.6 31.4 reduce-scatter.4

commit v2 on v0

--- a/solution.py
+++ b/solution.py
@@ -9,7 +9,7 @@
 from jax.sharding import PartitionSpec as P
 
 LANES = 128
-VMEM_LIMIT = 60 * 1024 * 1024
+VMEM_LIMIT = 125 * 512 * 1024
 GELU_SCALE = math.sqrt(2.0 / math.pi)
 
 
@@ -270,20 +270,17 @@
         def _():
             rows = width // shares
             me = position_ref[0]
-            for b in range(group):
-                part = total[b].T.astype(jnp.bfloat16)
-                for share in range(shares):
-                    mine = (me & 1) == (share & 1)
-                    place = (me >> 1) ^ (share >> 1)
-                    block = part[share * rows : (share + 1) * rows]
-
-                    @pl.when(mine)
-                    def _():
-                        keep_ref[place, b] = block
-
-                    @pl.when(jnp.logical_not(mine))
-                    def _():
-                        send_ref[place, b] = block
+            for parity in range(2):
+
+                @pl.when((me & 1) == parity)
+                def _():
+                    for b in range(group):
+                        part = total[b].T.astype(jnp.bfloat16)
+                        for share in range(shares):
+                            ref = keep_ref if share & 1 == parity else send_ref
+                            ref[(me >> 1) ^ (share >> 1), b] = part[
+                                share * rows : (share + 1) * rows
+                            ]
 
 
 def last_part(position, returned, unit, rows_of, grad_of, grad, shares):
@@ -377,11 +374,12 @@
 def other_hops(totals):
     total = jnp.concatenate(totals, axis=1)
     count = total.shape[0]
+    came = None
     while count > 1:
         count //= 2
         came = swap_with(total[count:].astype(jnp.bfloat16), 2 * count)
         total = total[:count] + came.astype(jnp.float32)
-    return total[0]
+    return total[0], came
 
 
 def scatter(part):
@@ -420,17 +418,19 @@
     layer, part_high, *back_high = middle_part(
         received[1], w_two, features, cotangent, layer, half, held, backs
     )
-    parts_two = [scatter(part_low), scatter(part_high)]
+    grad_two = jnp.concatenate([scatter(part_low), scatter(part_high)], axis=0).astype(
+        jnp.float32
+    )
     for index, array in enumerate(back_high):
-        before = (latest, parts_two) if index else latest
+        before = (latest, grad_two) if index else latest
         latest = back_high[index] = exchange(array, before)
 
-    grad, hops, parts_one = None, [], []
+    grad, hops, parts_one, came = None, [], [], None
     for index in range(units):
         final = units > 1 and index == units - 1
         back, at = (back_high[1], 0) if final else (back_high[0], index)
         if final:
-            back = after(back, parts_one)
+            back = after(back, parts_one[0])
         returned = [(back_low, index), (back, at)]
         grad_of = (w_one, cotangent)
         if final:
@@ -440,18 +440,18 @@
             keep, send, grad = last_part(
                 position, returned, index, features, grad_of, grad, shares
             )
+        if came is not None:
+            send = after(send, came)
         hops.append(first_hop(keep, send))
-        if index == units // 2 - 1 or index == units - 1:
-            parts_one.append(other_hops(hops[-(units // 2 or 1) :]))
-    parts_two = after(parts_two, hops[-1])
-    grad_one = jnp.concatenate(parts_one[:-1] + [jnp.zeros_like(parts_one[-1])], axis=0)
-    start = held - parts_one[-1].shape[0]
-    grad_one = lax.dynamic_update_slice(grad_one, parts_one[-1], (start, 0, 0))
+        if index >= units - 3 and index > 0 or units == 1:
+            part, came = other_hops(hops)
+            parts_one.append(part)
+            hops = []
     return (
         layer,
         grad,
-        grad_one,
-        jnp.concatenate(parts_two, axis=0).astype(jnp.float32),
+        jnp.concatenate(parts_one, axis=0),
+        grad_two,
     )
 
 

time: 828 us -> 825 us (level)
  transfers between devices with their start and end apart: 18 -> 19, of which waited for: 14 -> 13; matrix products, arithmetic and copies ran while one was open for 1% -> 1% of each run, Pallas kernels for 15% -> 14%
where the time goes in v2:
time: 825 us; the launch traced here: 824 us
  waiting for transfers between devices  488 us (59%)
  blocking collectives  143 us (17%)
  Pallas kernels  126 us (15%)
  starting transfers between devices  32.3 us (4%)
  other arithmetic  15.3 us (2%)
  between operations  13.9 us (2%)
    all_to_all x5, waiting for transfers between devices, exchange(): return lax.all_to_all(array, 'mp', split_axis=0, concat_axis=0, tiled=True)  325 us
    all_to_all x1, blocking collectives, exchange(): return lax.all_to_all(array, 'mp', split_axis=0, concat_axis=0, tiled=True)  143 us
    reduce_scatter x2, waiting for transfers between devices, scatter(): return lax.psum_scatter(part, 'dp', scatter_dimension=1, tiled=True)  70 us
    pallas_call x2, Pallas kernels, middle_part(): pl.pallas_call(functools.partial(middle_kernel, owners, group, sources, b...  59.4 us
    pallas_call x5, Pallas kernels, last_part(): pl.pallas_call(functools.partial(last_kernel, held, sources, shares, rows...  44.8 us
    all_gather x1, waiting for transfers between devices, on_device(): w_one = lax.all_gather(after(factor_one, head), 'dp', axis=1, tiled=True)  37.6 us
    all_gather x1, waiting for transfers between devices, on_device(): w_two = lax.all_gather(after(factor_two, w_one), 'dp', axis=1, tiled=True)  37.5 us
    all_to_all x5, starting transfers between devices, exchange(): return lax.all_to_all(array, 'mp', split_axis=0, concat_axis=0, tiled=True)  25.1 us
  transfers between devices with their start and end apart: 19, of which 13 were waited for; matrix products, arithmetic and copies ran while one was open for 1% of the time, Pallas kernels for 14%

profile of v2, /device:TPU:0, one launch (start us, length us, event | category | flops | bytes accessed | tf_op | source)
XLA Modules:
  0.0 823.9 jit_solution(13036984089326881957)
XLA Ops:
  8.1 3.0 collective-permute-start.1
  11.2 6.3 collective-permute-done.1.refs_2_
  19.7 6.6 first.2
  26.3 6.0 all-to-all-start
  33.1 37.6 %all-gather.3.cloned.1.call-done.refs_3_.refs_4_.refs_5_.refs_2_ = bf16[32,256,256]{2,1,0:T(8,128)(2,1)} async-done(((bf16[32,64,256]{2,1,0:T(8,128)(2,1)}), bf16[32,256,256]{2,1,0:T(8,128)(2,1)}) %all-gather.3.cloned.1.call-update) | async-done | bytes 4194320 | tf_op jit(solution)/shard_map/all_gather | solution.py:400
  70.7 14.7 %first.3 = (bf16[8,3,16,8,1024]{4,3,2,1,0:T(8,128)(2,1)}, bf16[8,3,16,8,1024]{4,3,2,1,0:T(8,128)(2,1)}) custom-call(bf16[1024,8192]{1,0:T(8,128)(2,1)} %refs_2_.8, bf16[1024,8192]{1,0:T(8,128)(2,1)} %refs_2_.8, bf16[1024,8192]{1,0:T(8,128)(2,1)} %refs_2_.8, bf16[32,256,256]{2,1,0:T(8,128)(2,1)} %all-gather.3.cloned.1.call-done.refs_3_.refs_4_.refs_5_.refs_2_, ...), custom_call_target="tpu_custom_call" | custom-call | flops 3221225472 | bytes 28311552 | tf_op jit(solution)/shard_map/first/pallas_call | solution.py:110
  85.5 40.5 %all-to-all-done.refs_0_ = bf16[8,1,32,8,1024]{4,3,2,1,0:T(8,128)(2,1)} async-done(((bf16[8,1,32,8,1024]{4,3,2,1,0:T(8,128)(2,1)}), bf16[8,1,32,8,1024]{4,3,2,1,0:T(8,128)(2,1)}, u32[]{:S(2)}, u32[]{:S(2)}) %all-to-all-start) | async-done | bytes 4194336 | tf_op jit(solution)/shard_map/all_to_all | solution.py:348
  125.9 143.2 %all_to_all.30.refs_1_ = bf16[8,3,16,8,1024]{4,3,2,1,0:T(8,128)(2,1)} all-to-all(bf16[8,3,16,8,1024]{4,3,2,1,0:T(8,128)(2,1)} %get-tuple-element.39), channel_id=1, replica_groups=mesh['dp'=4,'mp'=8] {'mp'}, dimensions={0} | all-to-all | bytes 12582912 | tf_op jit(solution)/shard_map/all_to_all | solution.py:348
  269.2 4.8 all-to-all-start.2
  274.7 37.5 %all-gather.5.cloned.1.call-done.refs_2_ = bf16[32,256,256]{2,1,0:T(8,128)(2,1)} async-done(((bf16[32,64,256]{2,1,0:T(8,128)(2,1)}), bf16[32,256,256]{2,1,0:T(8,128)(2,1)}) %all-gather.5.cloned.1.call-update) | async-done | bytes 4194320 | tf_op jit(solution)/shard_map/all_gather | solution.py:401
  312.2 29.6 %middle.2 = (bf16[1024,8192]{1,0:T(8,128)(2,1)}, bf16[16,256,256]{2,1,0:T(8,128)(2,1)}, bf16[8,4,16,8,1024]{4,3,2,1,0:T(8,128)(2,1)}) custom-call(bf16[8,1,32,8,1024]{4,3,2,1,0:T(8,128)(2,1)} %all-to-all-done.refs_0_, bf16[8,3,16,8,1024]{4,3,2,1,0:T(8,128)(2,1)} %all_to_all.30.refs_1_, bf16[32,256,256]{2,1,0:T(8,128)(2,1)} %all-gather.5.cloned.1.call-done.refs_2_, ...), custom_call_target="tpu_custom_call" | custom-call | flops 6442450944 | bytes 46137344 | tf_op jit(solution)/shard_map/middle/pallas_call | solution.py:199
  341.8 69.2 %all-to-all-done.2.refs_1_ = bf16[8,3,16,8,1024]{4,3,2,1,0:T(8,128)(2,1)} async-done(((bf16[8,3,16,8,1024]{4,3,2,1,0:T(8,128)(2,1)}), bf16[8,3,16,8,1024]{4,3,2,1,0:T(8,128)(2,1)}, u32[]{:S(2)}, u32[]{:S(2)}) %all-to-all-start.2) | async-done | bytes 6291488 | tf_op jit(solution)/shard_map/all_to_all | solution.py:348
  411.0 5.0 all-to-all-start.3
  416.0 29.8 %middle.3 = (bf16[1024,8192]{1,0:T(8,128)(2,1)}, bf16[16,256,256]{2,1,0:T(8,128)(2,1)}, bf16[8,3,16,8,1024]{4,3,2,1,0:T(8,128)(2,1)}, bf16[8,1,16,8,1024]{4,3,2,1,0:T(8,128)(2,1)}) custom-call(bf16[8,1,32,8,1024]{4,3,2,1,0:T(8,128)(2,1)} %all-to-all-done.refs_0_, ...), custom_call_target="tpu_custom_call", output_to_operand_aliasing={{0}: (5, {})} | custom-call | flops 6442450944 | bytes 46137344 | tf_op jit(solution)/shard_map/middle/pallas_call | solution.py:199
  445.8 152.1 %all-to-all-done.3.refs_0_ = bf16[8,4,16,8,1024]{4,3,2,1,0:T(8,128)(2,1)} async-done(((bf16[8,4,16,8,1024]{4,3,2,1,0:T(8,128)(2,1)}), bf16[8,4,16,8,1024]{4,3,2,1,0:T(8,128)(2,1)}, u32[]{:S(2)}, u32[]{:S(2)}) %all-to-all-start.3) | async-done | bytes 8388640 | tf_op jit(solution)/shard_map/all_to_all | solution.py:348
  598.0 4.8 all-to-all-start.4
  604.1 35.4 %reduce-scatter.3.cloned.1.call-done = bf16[16,64,256]{2,1,0:T(8,128)(2,1)} async-done(((bf16[16,256,256]{2,1,0:T(8,128)(2,1)}), bf16[16,64,256]{2,1,0:T(8,128)(2,1)}) %reduce-scatter.3.cloned.1.call-update) | async-done | bytes 524304 | tf_op jit(solution)/shard_map/reduce_scatter | solution.py:386
  639.5 34.6 %reduce-scatter.5.cloned.1.call-done = bf16[16,64,256]{2,1,0:T(8,128)(2,1)} async-done(((bf16[16,256,256]{2,1,0:T(8,128)(2,1)}), bf16[16,64,256]{2,1,0:T(8,128)(2,1)}) %reduce-scatter.5.cloned.1.call-update) | async-done | bytes 524304 | tf_op jit(solution)/shard_map/reduce_scatter | solution.py:386
  674.1 2.7 maximum_convert_fusion
  676.7 63.5 %all-to-all-done.4.refs_1_ = bf16[8,3,16,8,1024]{4,3,2,1,0:T(8,128)(2,1)} async-done(((bf16[8,3,16,8,1024]{4,3,2,1,0:T(8,128)(2,1)}), bf16[8,3,16,8,1024]{4,3,2,1,0:T(8,128)(2,1)}, u32[]{:S(2)}, u32[]{:S(2)}) %all-to-all-start.4) | async-done | bytes 6291488 | tf_op jit(solution)/shard_map/all_to_all | solution.py:348
  740.2 4.5 all-to-all-start.5
  744.7 10.1 %last.5 = (bf16[2,8,64,256]{3,2,1,0:T(8,128)(2,1)}, bf16[2,8,64,256]{3,2,1,0:T(8,128)(2,1)}, bf16[1024,8192]{1,0:T(8,128)(2,1)}) custom-call(s32[1]{0:T(128)} %bitcast.position_ref, bf16[8,4,16,8,1024]{4,3,2,1,0:T(8,128)(2,1)} %all-to-all-done.3.refs_0_, bf16[8,3,16,8,1024]{4,3,2,1,0:T(8,128)(2,1)} %all-to-all-done.4.refs_1_, bf16[1024,8192]{1,0:T(8,128)(2,1)} %refs_2_.8, ...), custom_call_target="tpu_custom_call" | custom-call | flops 2147483648 | bytes 16777216 | tf_op jit(solution)/shard_map/last/pallas_call | solution.py:322
  754.8 10.1 %last.6 = (bf16[2,8,64,256]{3,2,1,0:T(8,128)(2,1)}, bf16[2,8,64,256]{3,2,1,0:T(8,128)(2,1)}, bf16[1024,8192]{1,0:T(8,128)(2,1)}) custom-call(s32[1]{0:T(128)} %bitcast.position_ref, bf16[8,4,16,8,1024]{4,3,2,1,0:T(8,128)(2,1)} %all-to-all-done.3.refs_0_, bf16[8,3,16,8,1024]{4,3,2,1,0:T(8,128)(2,1)} %all-to-all-done.4.refs_1_, ...), custom_call_target="tpu_custom_call", output_to_operand_aliasing={{2}: (6, {})} | custom-call | flops 2147483648 | bytes 16777216 | tf_op jit(solution)/shard_map/last/pallas_call | solution.py:322
  770.6 1.5 collective-permute-start.5
  772.1 10.0 %last.7 = (bf16[2,8,64,256]{3,2,1,0:T(8,128)(2,1)}, bf16[2,8,64,256]{3,2,1,0:T(8,128)(2,1)}, bf16[1024,8192]{1,0:T(8,128)(2,1)}) custom-call(s32[1]{0:T(128)} %bitcast.position_ref, bf16[8,4,16,8,1024]{4,3,2,1,0:T(8,128)(2,1)} %all-to-all-done.3.refs_0_, bf16[8,3,16,8,1024]{4,3,2,1,0:T(8,128)(2,1)} %all-to-all-done.4.refs_1_, ...), custom_call_target="tpu_custom_call", output_to_operand_aliasing={{2}: (6, {})} | custom-call | flops 2147483648 | bytes 16777216 | tf_op jit(solution)/shard_map/last/pallas_call | solution.py:322
  782.1 2.6 collective-permute-done.5
  784.7 2.1 collective-permute-done.6
  791.3 2.3 fusion.2
  793.6 6.9 last.9
  800.5 2.1 collective-permute-done.8
  806.0 7.6 last.8
  814.8 2.5 pad_maximum_fusion
  (53 shorter events, 20.5 us)
Async XLA Ops:
  8.1 10.9 %copy-start.5 = (bf16[8,64,256]{2,1,0:T(8,128)(2,1)}, bf16[8,64,256]{2,1,0:T(8,128)(2,1)S(1)}, u32[]{:S(2)}) copy-start(bf16[8,64,256]{2,1,0:T(8,128)(2,1)S(1)} %slice.24.refs_0_) | copy-start | bytes 786436
  8.1 9.3 %collective-permute-start.1 = (bf16[8,64,256]{2,1,0:T(8,128)(2,1)S(1)}, bf16[8,64,256]{2,1,0:T(8,128)(2,1)S(1)}, u32[]{:S(2)}, u32[]{:S(2)}) collective-permute-start(bf16[8,64,256]{2,1,0:T(8,128)(2,1)S(1)} %slice.24.refs_0_), channel_id=1, source_target_pairs={{0,16},{8,24},{16,0},{24,8},{1,17},{9,25},{17,1},{25,9},{2,18},{10... | collective-permute-start | bytes 786440 | tf_op jit(solution)/shard_map/ppermute | solution.py:357
  11.2 6.3 collective-permute-start
  17.5 1.5 copy-start.7
  17.5 1.5 collective-permute-start.2
  17.5 1.5 copy-start.8
  19.0 0.7 copy-start.9
  26.3 99.6 %all-to-all-start = ((bf16[8,1,32,8,1024]{4,3,2,1,0:T(8,128)(2,1)}), bf16[8,1,32,8,1024]{4,3,2,1,0:T(8,128)(2,1)}, u32[]{:S(2)}, u32[]{:S(2)}) async-start(bf16[8,1,32,8,1024]{4,3,2,1,0:T(8,128)(2,1)} %first.2), calls=%async_computation | async-start | bytes 8388608 | tf_op jit(solution)/shard_map/all_to_all | solution.py:348
  32.4 38.3 %all-gather.3.cloned.1.call-start = ((), (), s32[]{:S(2)}) async-start(), calls=%async_computation.8 | async-start | bytes 5242880 | tf_op jit(solution)/shard_map/all_gather | solution.py:400
  269.2 141.9 %all-to-all-start.2 = ((bf16[8,3,16,8,1024]{4,3,2,1,0:T(8,128)(2,1)}), bf16[8,3,16,8,1024]{4,3,2,1,0:T(8,128)(2,1)}, u32[]{:S(2)}, u32[]{:S(2)}) async-start(bf16[8,3,16,8,1024]{4,3,2,1,0:T(8,128)(2,1)} %get-tuple-element.40), calls=%async_computation.2 | async-start | bytes 12582912 | tf_op jit(solution)/shard_map/all_to_all | solution.py:348
  273.9 38.3 %all-gather.5.cloned.1.call-start = ((), (), s32[]{:S(2)}) async-start(), calls=%async_computation.9 | async-start | bytes 5242880 | tf_op jit(solution)/shard_map/all_gather | solution.py:401
  411.0 187.0 %all-to-all-start.3 = ((bf16[8,4,16,8,1024]{4,3,2,1,0:T(8,128)(2,1)}), bf16[8,4,16,8,1024]{4,3,2,1,0:T(8,128)(2,1)}, u32[]{:S(2)}, u32[]{:S(2)}) async-start(bf16[8,4,16,8,1024]{4,3,2,1,0:T(8,128)(2,1)} %get-tuple-element.45), calls=%async_computation.3 | async-start | bytes 16777216 | tf_op jit(solution)/shard_map/all_to_all | solution.py:348
  598.0 142.2 %all-to-all-start.4 = ((bf16[8,3,16,8,1024]{4,3,2,1,0:T(8,128)(2,1)}), bf16[8,3,16,8,1024]{4,3,2,1,0:T(8,128)(2,1)}, u32[]{:S(2)}, u32[]{:S(2)}) async-start(bf16[8,3,16,8,1024]{4,3,2,1,0:T(8,128)(2,1)} %get-tuple-element.48), calls=%async_computation.4 | async-start | bytes 12582912 | tf_op jit(solution)/shard_map/all_to_all | solution.py:348
  602.8 36.7 %reduce-scatter.3.cloned.1.call-start = ((), (), s32[]{:S(2)}) async-start(), calls=%async_computation.10 | async-start | bytes 2621440 | tf_op jit(solution)/shard_map/reduce_scatter | solution.py:386
  603.5 70.6 %reduce-scatter.5.cloned.1.call-start = ((), (), s32[]{:S(2)}) async-start(), calls=%async_computation.11 | async-start | bytes 2621440 | tf_op jit(solution)/shard_map/reduce_scatter | solution.py:386
  740.2 53.4 %all-to-all-start.5 = ((bf16[8,1,16,8,1024]{4,3,2,1,0:T(8,128)(2,1)}), bf16[8,1,16,8,1024]{4,3,2,1,0:T(8,128)(2,1)}, u32[]{:S(2)}, u32[]{:S(2)}) async-start(bf16[8,1,16,8,1024]{4,3,2,1,0:T(8,128)(2,1)} %get-tuple-element.51), calls=%async_computation.7 | async-start | bytes 4194304 | tf_op jit(solution)/shard_map/all_to_all | solution.py:348
  754.8 10.6 %collective-permute-start.3 = (bf16[2,8,64,256]{3,2,1,0:T(8,128)(2,1)}, bf16[2,8,64,256]{3,2,1,0:T(8,128)(2,1)S(1)}, u32[]{:S(2)}, u32[]{:S(2)}) collective-permute-start(bf16[2,8,64,256]{3,2,1,0:T(8,128)(2,1)} %get-tuple-element.53), channel_id=1, source_target_pairs={{0,8},{8,0},{16,24},{24,16},{1,9},{9,1},{17,25},{25,17},{2,10},{10... | collective-permute-start | bytes 1572872 | tf_op jit(solution)/shard_map/ppermute | solution.py:357
  764.9 2.6 collective-permute-start.4
  765.4 0.8 copy-start.6
  768.7 1.0 copy-start
  770.6 14.2 %collective-permute-start.5 = (bf16[1,16,64,256]{3,2,1,0:T(8,128)(2,1)}, bf16[1,16,64,256]{3,2,1,0:T(8,128)(2,1)}, u32[]{:S(2)}, u32[]{:S(2)}) collective-permute-start(bf16[1,16,64,256]{3,2,1,0:T(8,128)(2,1)} %fusion.3), channel_id=1, source_target_pairs={{0,16},{8,24},{16,0},{24,8},{1,17},{9,25},{17,1},{25,9},{2,18},{10... | collective-permute-start | bytes 1572872 | tf_op jit(solution)/shard_map/ppermute | solution.py:357
  784.7 2.1 collective-permute-start.6
  788.0 1.0 copy-start.2
  789.7 10.8 %collective-permute-start.7 = (bf16[1,8,64,256]{3,2,1,0:T(8,128)(2,1)}, bf16[1,8,64,256]{3,2,1,0:T(8,128)(2,1)S(1)}, u32[]{:S(2)}, u32[]{:S(2)}) collective-permute-start(bf16[1,8,64,256]{3,2,1,0:T(8,128)(2,1)} %slice.56), channel_id=1, source_target_pairs={{0,16},{8,24},{16,0},{24,8},{1,17},{9,25},{17,1},{25,9},{2,18},{10... | collective-permute-start | bytes 786440 | tf_op jit(solution)/shard_map/ppermute | solution.py:357
  793.6 11.6 %copy-start.3 = (f32[2,8,64,256]{3,2,1,0:T(8,128)S(1)}, f32[2,8,64,256]{3,2,1,0:T(8,128)}, u32[]{:S(2)}) copy-start(f32[2,8,64,256]{3,2,1,0:T(8,128)} %copy-done.2) | copy-start | bytes 3145732
  800.5 2.1 collective-permute-start.8
  803.8 2.2 copy-start.4
  804.6 9.0 %collective-permute-start.9 = (bf16[1,8,64,256]{3,2,1,0:T(8,128)(2,1)}, bf16[1,8,64,256]{3,2,1,0:T(8,128)(2,1)}, u32[]{:S(2)}, u32[]{:S(2)}) collective-permute-start(bf16[1,8,64,256]{3,2,1,0:T(8,128)(2,1)} %slice.55), channel_id=1, source_target_pairs={{0,16},{8,24},{16,0},{24,8},{1,17},{9,25},{17,1},{25,9},{2,18},{10... | collective-permute-start | bytes 786440 | tf_op jit(solution)/shard_map/ppermute | solution.py:357
  806.0 8.8 %copy-start.1 = (f32[16,64,256]{2,1,0:T(8,128)S(1)}, f32[16,64,256]{2,1,0:T(8,128)}, u32[]{:S(2)}) copy-start(f32[16,64,256]{2,1,0:T(8,128)} %fusion.2) | copy-start | bytes 3145732
Sparse Core Ops, SparseCore 0:
  34.8 35.9 all-gather.2
  276.3 35.8 all-gather.4
  606.7 32.7 reduce-scatter.2
  642.6 31.4 reduce-scatter.4

commit v3 on v2

--- a/solution.py
+++ b/solution.py
@@ -368,18 +368,26 @@
 
 
 def first_hop(keep, send):
-    return keep.astype(jnp.float32) + swap_with(send, 1).astype(jnp.float32)
-
-
-def other_hops(totals):
-    total = jnp.concatenate(totals, axis=1)
-    count = total.shape[0]
+    return [keep, swap_with(send, 1)]
+
+
+def added(terms):
+    return sum((term.astype(jnp.float32) for term in terms[1:]), terms[0].astype(jnp.float32))
+
+
+def other_hops(sums):
+    group = sums[0][0].shape[1]
+    count = sums[0][0].shape[0]
     came = None
     while count > 1:
         count //= 2
-        came = swap_with(total[count:].astype(jnp.bfloat16), 2 * count)
-        total = total[:count] + came.astype(jnp.float32)
-    return total[0], came
+        leaving = [added([term[count:] for term in terms]).astype(jnp.bfloat16) for terms in sums]
+        came = swap_with(jnp.concatenate(leaving, axis=1), 2 * count)
+        sums = [
+            [term[:count] for term in terms] + [came[:, at * group : (at + 1) * group]]
+            for at, terms in enumerate(sums)
+        ]
+    return [added([term[0] for term in terms]) for terms in sums], came
 
 
 def scatter(part):
@@ -429,8 +437,6 @@
     for index in range(units):
         final = units > 1 and index == units - 1
         back, at = (back_high[1], 0) if final else (back_high[0], index)
-        if final:
-            back = after(back, parts_one[0])
         returned = [(back_low, index), (back, at)]
         grad_of = (w_one, cotangent)
         if final:
@@ -444,13 +450,17 @@
             send = after(send, came)
         hops.append(first_hop(keep, send))
         if index >= units - 3 and index > 0 or units == 1:
-            part, came = other_hops(hops)
-            parts_one.append(part)
+            parts, came = other_hops(hops)
+            parts_one += parts
             hops = []
+    empty = jnp.zeros((held,) + parts_one[0].shape[1:], jnp.float32)
+    grad_one = after(empty, back_low)
+    for index, part in enumerate(parts_one):
+        grad_one = lax.dynamic_update_slice(grad_one, part, (index * unit, 0, 0))
     return (
         layer,
         grad,
-        jnp.concatenate(parts_one, axis=0),
+        grad_one,
         grad_two,
     )
 

time: 825 us -> 825 us (level)
  transfers between devices with their start and end apart: 19 -> 19, of which waited for: 13 -> 14; matrix products, arithmetic and copies ran while one was open for 1% -> 2% of each run, Pallas kernels for 14% -> 14%
where the time goes in v3:
time: 825 us; the launch traced here: 824 us
  waiting for transfers between devices  490 us (59%)
  blocking collectives  143 us (17%)
  Pallas kernels  126 us (15%)
  starting transfers between devices  33.5 us (4%)
  other arithmetic  14.1 us (2%)
  between operations  13.9 us (2%)
    all_to_all x5, waiting for transfers between devices, exchange(): return lax.all_to_all(array, 'mp', split_axis=0, concat_axis=0, tiled=True)  328 us
    all_to_all x1, blocking collectives, exchange(): return lax.all_to_all(array, 'mp', split_axis=0, concat_axis=0, tiled=True)  143 us
    reduce_scatter x2, waiting for transfers between devices, scatter(): return lax.psum_scatter(part, 'dp', scatter_dimension=1, tiled=True)  70 us
    pallas_call x2, Pallas kernels, middle_part(): pl.pallas_call(functools.partial(middle_kernel, owners, group, sources, b...  59.4 us
    pallas_call x5, Pallas kernels, last_part(): pl.pallas_call(functools.partial(last_kernel, held, sources, shares, rows...  44.9 us
    all_gather x1, waiting for transfers between devices, on_device(): w_one = lax.all_gather(after(factor_one, head), 'dp', axis=1, tiled=True)  37.6 us
    all_gather x1, waiting for transfers between devices, on_device(): w_two = lax.all_gather(after(factor_two, w_one), 'dp', axis=1, tiled=True)  37.5 us
    all_to_all x5, starting transfers between devices, exchange(): return lax.all_to_all(array, 'mp', split_axis=0, concat_axis=0, tiled=True)  25.1 us
  transfers between devices with their start and end apart: 19, of which 14 were waited for; matrix products, arithmetic and copies ran while one was open for 2% of the time, Pallas kernels for 14%

profile of v3, /device:TPU:0, one launch (start us, length us, event | category | flops | bytes accessed | tf_op | source)
XLA Modules:
  0.0 824.1 jit_solution(5325555671664288826)
XLA Ops:
  8.1 3.0 collective-permute-start.1
  11.2 6.3 collective-permute-done.1.refs_2_
  19.7 6.6 first.2
  26.3 6.0 all-to-all-start
  33.1 37.6 %all-gather.3.cloned.1.call-done.refs_3_.refs_4_.refs_5_.refs_2_ = bf16[32,256,256]{2,1,0:T(8,128)(2,1)} async-done(((bf16[32,64,256]{2,1,0:T(8,128)(2,1)}), bf16[32,256,256]{2,1,0:T(8,128)(2,1)}) %all-gather.3.cloned.1.call-update) | async-done | bytes 4194320 | tf_op jit(solution)/shard_map/all_gather | solution.py:408
  70.7 14.8 %first.3 = (bf16[8,3,16,8,1024]{4,3,2,1,0:T(8,128)(2,1)}, bf16[8,3,16,8,1024]{4,3,2,1,0:T(8,128)(2,1)}) custom-call(bf16[1024,8192]{1,0:T(8,128)(2,1)} %refs_2_.8, bf16[1024,8192]{1,0:T(8,128)(2,1)} %refs_2_.8, bf16[1024,8192]{1,0:T(8,128)(2,1)} %refs_2_.8, bf16[32,256,256]{2,1,0:T(8,128)(2,1)} %all-gather.3.cloned.1.call-done.refs_3_.refs_4_.refs_5_.refs_2_, ...), custom_call_target="tpu_custom_call" | custom-call | flops 3221225472 | bytes 28311552 | tf_op jit(solution)/shard_map/first/pallas_call | solution.py:110
  85.5 40.5 %all-to-all-done.refs_0_ = bf16[8,1,32,8,1024]{4,3,2,1,0:T(8,128)(2,1)} async-done(((bf16[8,1,32,8,1024]{4,3,2,1,0:T(8,128)(2,1)}), bf16[8,1,32,8,1024]{4,3,2,1,0:T(8,128)(2,1)}, u32[]{:S(2)}, u32[]{:S(2)}) %all-to-all-start) | async-done | bytes 4194336 | tf_op jit(solution)/shard_map/all_to_all | solution.py:348
  125.9 143.2 %all_to_all.30.refs_1_ = bf16[8,3,16,8,1024]{4,3,2,1,0:T(8,128)(2,1)} all-to-all(bf16[8,3,16,8,1024]{4,3,2,1,0:T(8,128)(2,1)} %get-tuple-element.39), channel_id=1, replica_groups=mesh['dp'=4,'mp'=8] {'mp'}, dimensions={0} | all-to-all | bytes 12582912 | tf_op jit(solution)/shard_map/all_to_all | solution.py:348
  269.1 4.8 all-to-all-start.2
  274.7 37.5 %all-gather.5.cloned.1.call-done.refs_2_ = bf16[32,256,256]{2,1,0:T(8,128)(2,1)} async-done(((bf16[32,64,256]{2,1,0:T(8,128)(2,1)}), bf16[32,256,256]{2,1,0:T(8,128)(2,1)}) %all-gather.5.cloned.1.call-update) | async-done | bytes 4194320 | tf_op jit(solution)/shard_map/all_gather | solution.py:409
  312.2 29.6 %middle.2 = (bf16[1024,8192]{1,0:T(8,128)(2,1)}, bf16[16,256,256]{2,1,0:T(8,128)(2,1)}, bf16[8,4,16,8,1024]{4,3,2,1,0:T(8,128)(2,1)}) custom-call(bf16[8,1,32,8,1024]{4,3,2,1,0:T(8,128)(2,1)} %all-to-all-done.refs_0_, bf16[8,3,16,8,1024]{4,3,2,1,0:T(8,128)(2,1)} %all_to_all.30.refs_1_, bf16[32,256,256]{2,1,0:T(8,128)(2,1)} %all-gather.5.cloned.1.call-done.refs_2_, ...), custom_call_target="tpu_custom_call" | custom-call | flops 6442450944 | bytes 46137344 | tf_op jit(solution)/shard_map/middle/pallas_call | solution.py:199
  341.7 69.2 %all-to-all-done.2.refs_1_ = bf16[8,3,16,8,1024]{4,3,2,1,0:T(8,128)(2,1)} async-done(((bf16[8,3,16,8,1024]{4,3,2,1,0:T(8,128)(2,1)}), bf16[8,3,16,8,1024]{4,3,2,1,0:T(8,128)(2,1)}, u32[]{:S(2)}, u32[]{:S(2)}) %all-to-all-start.2) | async-done | bytes 6291488 | tf_op jit(solution)/shard_map/all_to_all | solution.py:348
  410.9 5.0 all-to-all-start.3
  415.9 29.8 %middle.3 = (bf16[1024,8192]{1,0:T(8,128)(2,1)}, bf16[16,256,256]{2,1,0:T(8,128)(2,1)}, bf16[8,3,16,8,1024]{4,3,2,1,0:T(8,128)(2,1)}, bf16[8,1,16,8,1024]{4,3,2,1,0:T(8,128)(2,1)}) custom-call(bf16[8,1,32,8,1024]{4,3,2,1,0:T(8,128)(2,1)} %all-to-all-done.refs_0_, ...), custom_call_target="tpu_custom_call", output_to_operand_aliasing={{0}: (5, {})} | custom-call | flops 6442450944 | bytes 46137344 | tf_op jit(solution)/shard_map/middle/pallas_call | solution.py:199
  445.7 152.1 %all-to-all-done.3.refs_0_ = bf16[8,4,16,8,1024]{4,3,2,1,0:T(8,128)(2,1)} async-done(((bf16[8,4,16,8,1024]{4,3,2,1,0:T(8,128)(2,1)}), bf16[8,4,16,8,1024]{4,3,2,1,0:T(8,128)(2,1)}, u32[]{:S(2)}, u32[]{:S(2)}) %all-to-all-start.3) | async-done | bytes 8388640 | tf_op jit(solution)/shard_map/all_to_all | solution.py:348
  597.8 4.8 all-to-all-start.4
  603.9 35.5 %reduce-scatter.3.cloned.1.call-done = bf16[16,64,256]{2,1,0:T(8,128)(2,1)} async-done(((bf16[16,256,256]{2,1,0:T(8,128)(2,1)}), bf16[16,64,256]{2,1,0:T(8,128)(2,1)}) %reduce-scatter.3.cloned.1.call-update) | async-done | bytes 524304 | tf_op jit(solution)/shard_map/reduce_scatter | solution.py:394
  639.4 34.6 %reduce-scatter.5.cloned.1.call-done = bf16[16,64,256]{2,1,0:T(8,128)(2,1)} async-done(((bf16[16,256,256]{2,1,0:T(8,128)(2,1)}), bf16[16,64,256]{2,1,0:T(8,128)(2,1)}) %reduce-scatter.5.cloned.1.call-update) | async-done | bytes 524304 | tf_op jit(solution)/shard_map/reduce_scatter | solution.py:394
  673.9 2.7 maximum_convert_fusion
  676.6 63.5 %all-to-all-done.4.refs_1_ = bf16[8,3,16,8,1024]{4,3,2,1,0:T(8,128)(2,1)} async-done(((bf16[8,3,16,8,1024]{4,3,2,1,0:T(8,128)(2,1)}), bf16[8,3,16,8,1024]{4,3,2,1,0:T(8,128)(2,1)}, u32[]{:S(2)}, u32[]{:S(2)}) %all-to-all-start.4) | async-done | bytes 6291488 | tf_op jit(solution)/shard_map/all_to_all | solution.py:348
  740.1 4.5 all-to-all-start.5
  744.6 10.1 %last.5 = (bf16[2,8,64,256]{3,2,1,0:T(8,128)(2,1)}, bf16[2,8,64,256]{3,2,1,0:T(8,128)(2,1)}, bf16[1024,8192]{1,0:T(8,128)(2,1)}) custom-call(s32[1]{0:T(128)} %bitcast.position_ref, bf16[8,4,16,8,1024]{4,3,2,1,0:T(8,128)(2,1)} %all-to-all-done.3.refs_0_, bf16[8,3,16,8,1024]{4,3,2,1,0:T(8,128)(2,1)} %all-to-all-done.4.refs_1_, bf16[1024,8192]{1,0:T(8,128)(2,1)} %refs_2_.8, ...), custom_call_target="tpu_custom_call" | custom-call | flops 2147483648 | bytes 16777216 | tf_op jit(solution)/shard_map/last/pallas_call | solution.py:322
  754.7 10.2 %last.6 = (bf16[2,8,64,256]{3,2,1,0:T(8,128)(2,1)}, bf16[2,8,64,256]{3,2,1,0:T(8,128)(2,1)}, bf16[1024,8192]{1,0:T(8,128)(2,1)}) custom-call(s32[1]{0:T(128)} %bitcast.position_ref, bf16[8,4,16,8,1024]{4,3,2,1,0:T(8,128)(2,1)} %all-to-all-done.3.refs_0_, bf16[8,3,16,8,1024]{4,3,2,1,0:T(8,128)(2,1)} %all-to-all-done.4.refs_1_, ...), custom_call_target="tpu_custom_call", output_to_operand_aliasing={{2}: (6, {})} | custom-call | flops 2147483648 | bytes 16777216 | tf_op jit(solution)/shard_map/last/pallas_call | solution.py:322
  771.5 10.0 %last.7 = (bf16[2,8,64,256]{3,2,1,0:T(8,128)(2,1)}, bf16[2,8,64,256]{3,2,1,0:T(8,128)(2,1)}, bf16[1024,8192]{1,0:T(8,128)(2,1)}) custom-call(s32[1]{0:T(128)} %bitcast.position_ref, bf16[8,4,16,8,1024]{4,3,2,1,0:T(8,128)(2,1)} %all-to-all-done.3.refs_0_, bf16[8,3,16,8,1024]{4,3,2,1,0:T(8,128)(2,1)} %all-to-all-done.4.refs_1_, ...), custom_call_target="tpu_custom_call", output_to_operand_aliasing={{2}: (6, {})} | custom-call | flops 2147483648 | bytes 16777216 | tf_op jit(solution)/shard_map/last/pallas_call | solution.py:322
  781.6 2.6 collective-permute-done.5
  784.2 2.1 collective-permute-done.6
  786.3 1.9 add_convert_fusion.1
  789.7 2.6 all-to-all-done.5.refs_1_
  792.3 6.9 last.9
  800.9 1.9 bitcast_dynamic-update-slice_fusion.3
  802.8 1.9 bitcast_dynamic-update-slice_fusion.2
  808.1 7.6 last.8
  (66 shorter events, 20.9 us)
Async XLA Ops:
  8.1 10.9 %copy-start = (bf16[8,64,256]{2,1,0:T(8,128)(2,1)}, bf16[8,64,256]{2,1,0:T(8,128)(2,1)S(1)}, u32[]{:S(2)}) copy-start(bf16[8,64,256]{2,1,0:T(8,128)(2,1)S(1)} %slice.57.refs_0_) | copy-start | bytes 786436
  8.1 9.3 %collective-permute-start.1 = (bf16[8,64,256]{2,1,0:T(8,128)(2,1)S(1)}, bf16[8,64,256]{2,1,0:T(8,128)(2,1)S(1)}, u32[]{:S(2)}, u32[]{:S(2)}) collective-permute-start(bf16[8,64,256]{2,1,0:T(8,128)(2,1)S(1)} %slice.57.refs_0_), channel_id=1, source_target_pairs={{0,16},{8,24},{16,0},{24,8},{1,17},{9,25},{17,1},{25,9},{2,18},{10... | collective-permute-start | bytes 786440 | tf_op jit(solution)/shard_map/ppermute | solution.py:357
  11.2 6.3 collective-permute-start
  17.5 1.5 copy-start.13
  17.5 1.5 collective-permute-start.2
  26.3 99.6 %all-to-all-start = ((bf16[8,1,32,8,1024]{4,3,2,1,0:T(8,128)(2,1)}), bf16[8,1,32,8,1024]{4,3,2,1,0:T(8,128)(2,1)}, u32[]{:S(2)}, u32[]{:S(2)}) async-start(bf16[8,1,32,8,1024]{4,3,2,1,0:T(8,128)(2,1)} %first.2), calls=%async_computation | async-start | bytes 8388608 | tf_op jit(solution)/shard_map/all_to_all | solution.py:348
  32.4 38.3 %all-gather.3.cloned.1.call-start = ((), (), s32[]{:S(2)}) async-start(), calls=%async_computation.8 | async-start | bytes 5242880 | tf_op jit(solution)/shard_map/all_gather | solution.py:408
  269.1 141.8 %all-to-all-start.2 = ((bf16[8,3,16,8,1024]{4,3,2,1,0:T(8,128)(2,1)}), bf16[8,3,16,8,1024]{4,3,2,1,0:T(8,128)(2,1)}, u32[]{:S(2)}, u32[]{:S(2)}) async-start(bf16[8,3,16,8,1024]{4,3,2,1,0:T(8,128)(2,1)} %get-tuple-element.40), calls=%async_computation.2 | async-start | bytes 12582912 | tf_op jit(solution)/shard_map/all_to_all | solution.py:348
  273.9 38.3 %all-gather.5.cloned.1.call-start = ((), (), s32[]{:S(2)}) async-start(), calls=%async_computation.9 | async-start | bytes 5242880 | tf_op jit(solution)/shard_map/all_gather | solution.py:409
  410.9 186.9 %all-to-all-start.3 = ((bf16[8,4,16,8,1024]{4,3,2,1,0:T(8,128)(2,1)}), bf16[8,4,16,8,1024]{4,3,2,1,0:T(8,128)(2,1)}, u32[]{:S(2)}, u32[]{:S(2)}) async-start(bf16[8,4,16,8,1024]{4,3,2,1,0:T(8,128)(2,1)} %get-tuple-element.45), calls=%async_computation.3 | async-start | bytes 16777216 | tf_op jit(solution)/shard_map/all_to_all | solution.py:348
  597.8 142.3 %all-to-all-start.4 = ((bf16[8,3,16,8,1024]{4,3,2,1,0:T(8,128)(2,1)}), bf16[8,3,16,8,1024]{4,3,2,1,0:T(8,128)(2,1)}, u32[]{:S(2)}, u32[]{:S(2)}) async-start(bf16[8,3,16,8,1024]{4,3,2,1,0:T(8,128)(2,1)} %get-tuple-element.48), calls=%async_computation.4 | async-start | bytes 12582912 | tf_op jit(solution)/shard_map/all_to_all | solution.py:348
  602.6 36.8 %reduce-scatter.3.cloned.1.call-start = ((), (), s32[]{:S(2)}) async-start(), calls=%async_computation.10 | async-start | bytes 2621440 | tf_op jit(solution)/shard_map/reduce_scatter | solution.py:394
  603.3 70.6 %reduce-scatter.5.cloned.1.call-start = ((), (), s32[]{:S(2)}) async-start(), calls=%async_computation.11 | async-start | bytes 2621440 | tf_op jit(solution)/shard_map/reduce_scatter | solution.py:394
  740.1 52.3 %all-to-all-start.5 = ((bf16[8,1,16,8,1024]{4,3,2,1,0:T(8,128)(2,1)}), bf16[8,1,16,8,1024]{4,3,2,1,0:T(8,128)(2,1)}, u32[]{:S(2)}, u32[]{:S(2)}) async-start(bf16[8,1,16,8,1024]{4,3,2,1,0:T(8,128)(2,1)} %get-tuple-element.51), calls=%async_computation.7 | async-start | bytes 4194304 | tf_op jit(solution)/shard_map/all_to_all | solution.py:348
  754.7 10.2 %copy-start.16 = (bf16[2,8,64,256]{3,2,1,0:T(8,128)(2,1)S(1)}, bf16[2,8,64,256]{3,2,1,0:T(8,128)(2,1)}, u32[]{:S(2)}) copy-start(bf16[2,8,64,256]{3,2,1,0:T(8,128)(2,1)} %get-tuple-element.57) | copy-start | bytes 1572868
  754.7 14.3 %copy-start.1 = (bf16[2,8,64,256]{3,2,1,0:T(8,128)(2,1)S(1)}, bf16[2,8,64,256]{3,2,1,0:T(8,128)(2,1)}, u32[]{:S(2)}) copy-start(bf16[2,8,64,256]{3,2,1,0:T(8,128)(2,1)} %get-tuple-element.56) | copy-start | bytes 1572868
  764.9 2.1 collective-permute-start.4
  764.9 3.3 collective-permute-start.3
  770.0 14.2 %collective-permute-start.5 = (bf16[1,16,64,256]{3,2,1,0:T(8,128)(2,1)}, bf16[1,16,64,256]{3,2,1,0:T(8,128)(2,1)S(1)}, u32[]{:S(2)}, u32[]{:S(2)}) collective-permute-start(bf16[1,16,64,256]{3,2,1,0:T(8,128)(2,1)} %pad_maximum_fusion), channel_id=1, source_target_pairs={{0,16},{8,24},{16,0},{24,8},{1,17},{9,25},{17,1},{25,9},{2,18},{10... | collective-permute-start | bytes 1572872 | tf_op jit(solution)/shard_map/ppermute | solution.py:357
  784.2 2.1 copy-start.6
  784.2 2.1 collective-permute-start.6
  786.3 1.9 copy-start.7
  788.2 14.6 %copy-start.2 = (bf16[2,8,64,256]{3,2,1,0:T(8,128)(2,1)S(1)}, bf16[2,8,64,256]{3,2,1,0:T(8,128)(2,1)}, u32[]{:S(2)}) copy-start(bf16[2,8,64,256]{3,2,1,0:T(8,128)(2,1)} %get-tuple-element.58) | copy-start | bytes 1572868
  788.2 11.1 %collective-permute-start.7 = (bf16[1,8,64,256]{3,2,1,0:T(8,128)(2,1)}, bf16[1,8,64,256]{3,2,1,0:T(8,128)(2,1)S(1)}, u32[]{:S(2)}, u32[]{:S(2)}) collective-permute-start(bf16[1,8,64,256]{3,2,1,0:T(8,128)(2,1)} %add_convert_fusion.1), channel_id=1, source_target_pairs={{0,16},{8,24},{16,0},{24,8},{1,17},{9,25},{17,1},{25,9},{2,18},{10... | collective-permute-start | bytes 786440 | tf_op jit(solution)/shard_map/ppermute | solution.py:357
  799.2 5.5 copy-start.9
  799.2 7.9 copy-start.5
  799.2 7.9 copy-start.8
  799.3 5.5 collective-permute-start.8
  804.7 3.3 copy-start.11
  805.6 10.1 %collective-permute-start.9 = (bf16[1,8,64,256]{3,2,1,0:T(8,128)(2,1)}, bf16[1,8,64,256]{3,2,1,0:T(8,128)(2,1)}, u32[]{:S(2)}, u32[]{:S(2)}) collective-permute-start(bf16[1,8,64,256]{3,2,1,0:T(8,128)(2,1)} %add_convert_fusion), channel_id=1, source_target_pairs={{0,16},{8,24},{16,0},{24,8},{1,17},{9,25},{17,1},{25,9},{2,18},{10... | collective-permute-start | bytes 786440 | tf_op jit(solution)/shard_map/ppermute | solution.py:357
  808.1 7.7 copy-start.10
  808.1 7.7 copy-start.12
  (4 other events, 4.2 us)
Sparse Core Ops, SparseCore 0:
  34.8 35.8 all-gather.2
  276.3 35.8 all-gather.4
  606.5 32.8 reduce-scatter.2
  642.5 31.3 reduce-scatter.4

commit v4 on v3

--- a/solution.py
+++ b/solution.py
@@ -429,9 +429,11 @@
     grad_two = jnp.concatenate([scatter(part_low), scatter(part_high)], axis=0).astype(
         jnp.float32
     )
+    grad_one = factor_one.astype(jnp.float32)
     for index, array in enumerate(back_high):
-        before = (latest, grad_two) if index else latest
-        latest = back_high[index] = exchange(array, before)
+        if index:
+            array, grad_one, grad_two = lax.optimization_barrier((array, grad_one, grad_two))
+        latest = back_high[index] = exchange(array, latest)
 
     grad, hops, parts_one, came = None, [], [], None
     for index in range(units):
@@ -440,6 +442,9 @@
         returned = [(back_low, index), (back, at)]
         grad_of = (w_one, cotangent)
         if final:
+            grad_one = lax.dynamic_update_slice(grad_one, parts_one[0], (0, 0, 0))
+            back = after(back, grad_one)
+            returned = [(back_low, index), (back, at)]
             keep, send = last_part(position, returned, index, features, None, None, shares)
             (grad,) = last_part(position, returned, index, None, grad_of, grad, shares)
         else:
@@ -453,10 +458,9 @@
             parts, came = other_hops(hops)
             parts_one += parts
             hops = []
-    empty = jnp.zeros((held,) + parts_one[0].shape[1:], jnp.float32)
-    grad_one = after(empty, back_low)
     for index, part in enumerate(parts_one):
-        grad_one = lax.dynamic_update_slice(grad_one, part, (index * unit, 0, 0))
+        if index or units == 1:
+            grad_one = lax.dynamic_update_slice(grad_one, part, (index * unit, 0, 0))
     return (
         layer,
         grad,

time: 825 us -> 823 us (level)
  transfers between devices with their start and end apart: 19 -> 19, of which waited for: 14 -> 15; matrix products, arithmetic and copies ran while one was open for 2% -> 2% of each run, Pallas kernels for 14% -> 14%
where the time goes in v4:
time: 823 us; the launch traced here: 822 us
  waiting for transfers between devices  487 us (59%)
  blocking collectives  143 us (17%)
  Pallas kernels  125 us (15%)
  starting transfers between devices  33.3 us (4%)
  other arithmetic  17.6 us (2%)
  between operations  13.9 us (2%)
    all_to_all x5, waiting for transfers between devices, exchange(): return lax.all_to_all(array, 'mp', split_axis=0, concat_axis=0, tiled=True)  327 us
    all_to_all x1, blocking collectives, exchange(): return lax.all_to_all(array, 'mp', split_axis=0, concat_axis=0, tiled=True)  143 us
    reduce_scatter x2, waiting for transfers between devices, scatter(): return lax.psum_scatter(part, 'dp', scatter_dimension=1, tiled=True)  67.8 us
    pallas_call x2, Pallas kernels, middle_part(): pl.pallas_call(functools.partial(middle_kernel, owners, group, sources, b...  59.4 us
    pallas_call x5, Pallas kernels, last_part(): pl.pallas_call(functools.partial(last_kernel, held, sources, shares, rows...  44.8 us
    all_gather x1, waiting for transfers between devices, on_device(): w_one = lax.all_gather(after(factor_one, head), 'dp', axis=1, tiled=True)  37.6 us
    all_gather x1, waiting for transfers between devices, on_device(): w_two = lax.all_gather(after(factor_two, w_one), 'dp', axis=1, tiled=True)  37.5 us
    all_to_all x5, starting transfers between devices, exchange(): return lax.all_to_all(array, 'mp', split_axis=0, concat_axis=0, tiled=True)  25 us
  transfers between devices with their start and end apart: 19, of which 15 were waited for; matrix products, arithmetic and copies ran while one was open for 2% of the time, Pallas kernels for 14%

profile of v4, /device:TPU:0, one launch (start us, length us, event | category | flops | bytes accessed | tf_op | source)
XLA Modules:
  0.0 821.9 jit_solution(15685336761040888773)
XLA Ops:
  8.1 3.0 collective-permute-start.1
  11.2 6.3 collective-permute-done.1.refs_2_
  19.7 6.6 first.2
  26.3 6.0 all-to-all-start
  33.1 37.6 %all-gather.3.cloned.1.call-done.refs_3_.refs_4_.refs_5_.refs_2_ = bf16[32,256,256]{2,1,0:T(8,128)(2,1)} async-done(((bf16[32,64,256]{2,1,0:T(8,128)(2,1)}), bf16[32,256,256]{2,1,0:T(8,128)(2,1)}) %all-gather.3.cloned.1.call-update) | async-done | bytes 4194320 | tf_op jit(solution)/shard_map/all_gather | solution.py:408
  70.7 14.7 %first.3 = (bf16[8,3,16,8,1024]{4,3,2,1,0:T(8,128)(2,1)}, bf16[8,3,16,8,1024]{4,3,2,1,0:T(8,128)(2,1)}) custom-call(bf16[1024,8192]{1,0:T(8,128)(2,1)} %refs_2_.8, bf16[1024,8192]{1,0:T(8,128)(2,1)} %refs_2_.8, bf16[1024,8192]{1,0:T(8,128)(2,1)} %refs_2_.8, bf16[32,256,256]{2,1,0:T(8,128)(2,1)} %all-gather.3.cloned.1.call-done.refs_3_.refs_4_.refs_5_.refs_2_, ...), custom_call_target="tpu_custom_call" | custom-call | flops 3221225472 | bytes 28311552 | tf_op jit(solution)/shard_map/first/pallas_call | solution.py:110
  85.4 40.5 %all-to-all-done.refs_0_ = bf16[8,1,32,8,1024]{4,3,2,1,0:T(8,128)(2,1)} async-done(((bf16[8,1,32,8,1024]{4,3,2,1,0:T(8,128)(2,1)}), bf16[8,1,32,8,1024]{4,3,2,1,0:T(8,128)(2,1)}, u32[]{:S(2)}, u32[]{:S(2)}) %all-to-all-start) | async-done | bytes 4194336 | tf_op jit(solution)/shard_map/all_to_all | solution.py:348
  125.9 143.2 %all_to_all.30.refs_1_ = bf16[8,3,16,8,1024]{4,3,2,1,0:T(8,128)(2,1)} all-to-all(bf16[8,3,16,8,1024]{4,3,2,1,0:T(8,128)(2,1)} %get-tuple-element.42), channel_id=1, replica_groups=mesh['dp'=4,'mp'=8] {'mp'}, dimensions={0} | all-to-all | bytes 12582912 | tf_op jit(solution)/shard_map/all_to_all | solution.py:348
  269.1 4.8 all-to-all-start.2
  274.7 37.5 %all-gather.5.cloned.1.call-done.refs_2_ = bf16[32,256,256]{2,1,0:T(8,128)(2,1)} async-done(((bf16[32,64,256]{2,1,0:T(8,128)(2,1)}), bf16[32,256,256]{2,1,0:T(8,128)(2,1)}) %all-gather.5.cloned.1.call-update) | async-done | bytes 4194320 | tf_op jit(solution)/shard_map/all_gather | solution.py:409
  312.2 29.6 %middle.2 = (bf16[1024,8192]{1,0:T(8,128)(2,1)}, bf16[16,256,256]{2,1,0:T(8,128)(2,1)}, bf16[8,4,16,8,1024]{4,3,2,1,0:T(8,128)(2,1)}) custom-call(bf16[8,1,32,8,1024]{4,3,2,1,0:T(8,128)(2,1)} %all-to-all-done.refs_0_, bf16[8,3,16,8,1024]{4,3,2,1,0:T(8,128)(2,1)} %all_to_all.30.refs_1_, bf16[32,256,256]{2,1,0:T(8,128)(2,1)} %all-gather.5.cloned.1.call-done.refs_2_, ...), custom_call_target="tpu_custom_call" | custom-call | flops 6442450944 | bytes 46137344 | tf_op jit(solution)/shard_map/middle/pallas_call | solution.py:199
  341.7 69.2 %all-to-all-done.2.refs_1_ = bf16[8,3,16,8,1024]{4,3,2,1,0:T(8,128)(2,1)} async-done(((bf16[8,3,16,8,1024]{4,3,2,1,0:T(8,128)(2,1)}), bf16[8,3,16,8,1024]{4,3,2,1,0:T(8,128)(2,1)}, u32[]{:S(2)}, u32[]{:S(2)}) %all-to-all-start.2) | async-done | bytes 6291488 | tf_op jit(solution)/shard_map/all_to_all | solution.py:348
  411.0 5.0 all-to-all-start.3
  415.9 29.8 %middle.3 = (bf16[1024,8192]{1,0:T(8,128)(2,1)}, bf16[16,256,256]{2,1,0:T(8,128)(2,1)}, bf16[8,3,16,8,1024]{4,3,2,1,0:T(8,128)(2,1)}, bf16[8,1,16,8,1024]{4,3,2,1,0:T(8,128)(2,1)}) custom-call(bf16[8,1,32,8,1024]{4,3,2,1,0:T(8,128)(2,1)} %all-to-all-done.refs_0_, ...), custom_call_target="tpu_custom_call", output_to_operand_aliasing={{0}: (5, {})} | custom-call | flops 6442450944 | bytes 46137344 | tf_op jit(solution)/shard_map/middle/pallas_call | solution.py:199
  445.8 152.2 %all-to-all-done.3.refs_0_ = bf16[8,4,16,8,1024]{4,3,2,1,0:T(8,128)(2,1)} async-done(((bf16[8,4,16,8,1024]{4,3,2,1,0:T(8,128)(2,1)}), bf16[8,4,16,8,1024]{4,3,2,1,0:T(8,128)(2,1)}, u32[]{:S(2)}, u32[]{:S(2)}) %all-to-all-start.3) | async-done | bytes 8388640 | tf_op jit(solution)/shard_map/all_to_all | solution.py:348
  597.9 4.8 all-to-all-start.4
  605.6 33.8 %reduce-scatter.3.cloned.1.call-done = bf16[16,64,256]{2,1,0:T(8,128)(2,1)} async-done(((bf16[16,256,256]{2,1,0:T(8,128)(2,1)}), bf16[16,64,256]{2,1,0:T(8,128)(2,1)}) %reduce-scatter.3.cloned.1.call-update) | async-done | bytes 524304 | tf_op jit(solution)/shard_map/reduce_scatter | solution.py:394
  639.4 34.0 %reduce-scatter.5.cloned.1.call-done = bf16[16,64,256]{2,1,0:T(8,128)(2,1)} async-done(((bf16[16,256,256]{2,1,0:T(8,128)(2,1)}), bf16[16,64,256]{2,1,0:T(8,128)(2,1)}) %reduce-scatter.5.cloned.1.call-update) | async-done | bytes 524304 | tf_op jit(solution)/shard_map/reduce_scatter | solution.py:394
  673.5 2.7 maximum_convert_fusion
  676.1 64.0 %all-to-all-done.4.refs_1_ = bf16[8,3,16,8,1024]{4,3,2,1,0:T(8,128)(2,1)} async-done(((bf16[8,3,16,8,1024]{4,3,2,1,0:T(8,128)(2,1)}), bf16[8,3,16,8,1024]{4,3,2,1,0:T(8,128)(2,1)}, u32[]{:S(2)}, u32[]{:S(2)}) %all-to-all-start.4) | async-done | bytes 6291488 | tf_op jit(solution)/shard_map/all_to_all | solution.py:348
  740.2 4.5 all-to-all-start.5
  744.7 10.1 %last.5 = (bf16[2,8,64,256]{3,2,1,0:T(8,128)(2,1)}, bf16[2,8,64,256]{3,2,1,0:T(8,128)(2,1)}, bf16[1024,8192]{1,0:T(8,128)(2,1)}) custom-call(s32[1]{0:T(128)} %bitcast.position_ref, bf16[8,4,16,8,1024]{4,3,2,1,0:T(8,128)(2,1)} %all-to-all-done.3.refs_0_, bf16[8,3,16,8,1024]{4,3,2,1,0:T(8,128)(2,1)} %all-to-all-done.4.refs_1_, bf16[1024,8192]{1,0:T(8,128)(2,1)} %refs_2_.8, ...), custom_call_target="tpu_custom_call" | custom-call | flops 2147483648 | bytes 16777216 | tf_op jit(solution)/shard_map/last/pallas_call | solution.py:322
  754.8 10.1 %last.6 = (bf16[2,8,64,256]{3,2,1,0:T(8,128)(2,1)}, bf16[2,8,64,256]{3,2,1,0:T(8,128)(2,1)}, bf16[1024,8192]{1,0:T(8,128)(2,1)}) custom-call(s32[1]{0:T(128)} %bitcast.position_ref, bf16[8,4,16,8,1024]{4,3,2,1,0:T(8,128)(2,1)} %all-to-all-done.3.refs_0_, bf16[8,3,16,8,1024]{4,3,2,1,0:T(8,128)(2,1)} %all-to-all-done.4.refs_1_, ...), custom_call_target="tpu_custom_call", output_to_operand_aliasing={{2}: (6, {})} | custom-call | flops 2147483648 | bytes 16777216 | tf_op jit(solution)/shard_map/last/pallas_call | solution.py:322
  770.6 10.1 %last.7 = (bf16[2,8,64,256]{3,2,1,0:T(8,128)(2,1)}, bf16[2,8,64,256]{3,2,1,0:T(8,128)(2,1)}, bf16[1024,8192]{1,0:T(8,128)(2,1)}) custom-call(s32[1]{0:T(128)} %bitcast.position_ref, bf16[8,4,16,8,1024]{4,3,2,1,0:T(8,128)(2,1)} %all-to-all-done.3.refs_0_, bf16[8,3,16,8,1024]{4,3,2,1,0:T(8,128)(2,1)} %all-to-all-done.4.refs_1_, ...), custom_call_target="tpu_custom_call", output_to_operand_aliasing={{2}: (6, {})} | custom-call | flops 2147483648 | bytes 16777216 | tf_op jit(solution)/shard_map/last/pallas_call | solution.py:322
  780.7 2.9 collective-permute-done.5
  783.6 2.1 collective-permute-done.6
  785.7 1.9 add_convert_fusion.1
  789.1 1.9 bitcast_dynamic-update-slice_fusion.3
  792.4 6.8 last.9
  801.4 1.9 add_convert_fusion
  804.8 7.7 last.8
  813.4 2.0 bitcast_dynamic-update-slice_fusion
  (54 shorter events, 20.6 us)
Async XLA Ops:
  8.1 10.9 %copy-start.1 = (bf16[8,64,256]{2,1,0:T(8,128)(2,1)}, bf16[8,64,256]{2,1,0:T(8,128)(2,1)S(1)}, u32[]{:S(2)}) copy-start(bf16[8,64,256]{2,1,0:T(8,128)(2,1)S(1)} %slice.57.refs_0_) | copy-start | bytes 786436
  8.1 9.3 %collective-permute-start.1 = (bf16[8,64,256]{2,1,0:T(8,128)(2,1)S(1)}, bf16[8,64,256]{2,1,0:T(8,128)(2,1)S(1)}, u32[]{:S(2)}, u32[]{:S(2)}) collective-permute-start(bf16[8,64,256]{2,1,0:T(8,128)(2,1)S(1)} %slice.57.refs_0_), channel_id=1, source_target_pairs={{0,16},{8,24},{16,0},{24,8},{1,17},{9,25},{17,1},{25,9},{2,18},{10... | collective-permute-start | bytes 786440 | tf_op jit(solution)/shard_map/ppermute | solution.py:357
  11.2 6.3 collective-permute-start
  17.5 1.5 copy-start.8
  17.5 1.5 collective-permute-start.2
  17.5 1.5 copy-start.9
  19.0 0.7 copy-start.10
  26.3 99.6 %all-to-all-start = ((bf16[8,1,32,8,1024]{4,3,2,1,0:T(8,128)(2,1)}), bf16[8,1,32,8,1024]{4,3,2,1,0:T(8,128)(2,1)}, u32[]{:S(2)}, u32[]{:S(2)}) async-start(bf16[8,1,32,8,1024]{4,3,2,1,0:T(8,128)(2,1)} %first.2), calls=%async_computation | async-start | bytes 8388608 | tf_op jit(solution)/shard_map/all_to_all | solution.py:348
  32.3 38.3 %all-gather.3.cloned.1.call-start = ((), (), s32[]{:S(2)}) async-start(), calls=%async_computation.8 | async-start | bytes 5242880 | tf_op jit(solution)/shard_map/all_gather | solution.py:408
  269.1 141.8 %all-to-all-start.2 = ((bf16[8,3,16,8,1024]{4,3,2,1,0:T(8,128)(2,1)}), bf16[8,3,16,8,1024]{4,3,2,1,0:T(8,128)(2,1)}, u32[]{:S(2)}, u32[]{:S(2)}) async-start(bf16[8,3,16,8,1024]{4,3,2,1,0:T(8,128)(2,1)} %get-tuple-element.43), calls=%async_computation.2 | async-start | bytes 12582912 | tf_op jit(solution)/shard_map/all_to_all | solution.py:348
  273.9 38.3 %all-gather.5.cloned.1.call-start = ((), (), s32[]{:S(2)}) async-start(), calls=%async_computation.9 | async-start | bytes 5242880 | tf_op jit(solution)/shard_map/all_gather | solution.py:409
  411.0 187.0 %all-to-all-start.3 = ((bf16[8,4,16,8,1024]{4,3,2,1,0:T(8,128)(2,1)}), bf16[8,4,16,8,1024]{4,3,2,1,0:T(8,128)(2,1)}, u32[]{:S(2)}, u32[]{:S(2)}) async-start(bf16[8,4,16,8,1024]{4,3,2,1,0:T(8,128)(2,1)} %get-tuple-element.48), calls=%async_computation.3 | async-start | bytes 16777216 | tf_op jit(solution)/shard_map/all_to_all | solution.py:348
  597.9 142.2 %all-to-all-start.4 = ((bf16[8,3,16,8,1024]{4,3,2,1,0:T(8,128)(2,1)}), bf16[8,3,16,8,1024]{4,3,2,1,0:T(8,128)(2,1)}, u32[]{:S(2)}, u32[]{:S(2)}) async-start(bf16[8,3,16,8,1024]{4,3,2,1,0:T(8,128)(2,1)} %get-tuple-element.54), calls=%async_computation.6 | async-start | bytes 12582912 | tf_op jit(solution)/shard_map/all_to_all | solution.py:348
  602.7 1.3 copy-start
  602.7 36.7 %reduce-scatter.3.cloned.1.call-start = ((), (), s32[]{:S(2)}) async-start(), calls=%async_computation.10 | async-start | bytes 2621440 | tf_op jit(solution)/shard_map/reduce_scatter | solution.py:394
  603.5 70.0 %reduce-scatter.5.cloned.1.call-start = ((), (), s32[]{:S(2)}) async-start(), calls=%async_computation.11 | async-start | bytes 2621440 | tf_op jit(solution)/shard_map/reduce_scatter | solution.py:394
  740.2 52.3 %all-to-all-start.5 = ((bf16[8,1,16,8,1024]{4,3,2,1,0:T(8,128)(2,1)}), bf16[8,1,16,8,1024]{4,3,2,1,0:T(8,128)(2,1)}, u32[]{:S(2)}, u32[]{:S(2)}) async-start(bf16[8,1,16,8,1024]{4,3,2,1,0:T(8,128)(2,1)} %get-tuple-element.55), calls=%async_computation.7 | async-start | bytes 4194304 | tf_op jit(solution)/shard_map/all_to_all | solution.py:348
  754.8 10.7 %collective-permute-start.3 = (bf16[2,8,64,256]{3,2,1,0:T(8,128)(2,1)}, bf16[2,8,64,256]{3,2,1,0:T(8,128)(2,1)}, u32[]{:S(2)}, u32[]{:S(2)}) collective-permute-start(bf16[2,8,64,256]{3,2,1,0:T(8,128)(2,1)} %get-tuple-element.58), channel_id=1, source_target_pairs={{0,8},{8,0},{16,24},{24,16},{1,9},{9,1},{17,25},{25,17},{2,10},{10... | collective-permute-start | bytes 1572872 | tf_op jit(solution)/shard_map/ppermute | solution.py:357
  754.8 10.7 %copy-start.4 = (bf16[2,8,64,256]{3,2,1,0:T(8,128)(2,1)S(1)}, bf16[2,8,64,256]{3,2,1,0:T(8,128)(2,1)}, u32[]{:S(2)}) copy-start(bf16[2,8,64,256]{3,2,1,0:T(8,128)(2,1)} %get-tuple-element.57) | copy-start | bytes 1572868
  764.9 2.3 collective-permute-start.4
  769.1 14.5 %collective-permute-start.5 = (bf16[1,16,64,256]{3,2,1,0:T(8,128)(2,1)}, bf16[1,16,64,256]{3,2,1,0:T(8,128)(2,1)}, u32[]{:S(2)}, u32[]{:S(2)}) collective-permute-start(bf16[1,16,64,256]{3,2,1,0:T(8,128)(2,1)} %pad_maximum_fusion), channel_id=1, source_target_pairs={{0,16},{8,24},{16,0},{24,8},{1,17},{9,25},{17,1},{25,9},{2,18},{10... | collective-permute-start | bytes 1572872 | tf_op jit(solution)/shard_map/ppermute | solution.py:357
  783.6 2.1 collective-permute-start.6
  785.7 3.4 copy-start.5
  787.6 11.6 %collective-permute-start.7 = (bf16[1,8,64,256]{3,2,1,0:T(8,128)(2,1)}, bf16[1,8,64,256]{3,2,1,0:T(8,128)(2,1)S(1)}, u32[]{:S(2)}, u32[]{:S(2)}) collective-permute-start(bf16[1,8,64,256]{3,2,1,0:T(8,128)(2,1)} %add_convert_fusion.1), channel_id=1, source_target_pairs={{0,16},{8,24},{16,0},{24,8},{1,17},{9,25},{17,1},{25,9},{2,18},{10... | collective-permute-start | bytes 786440 | tf_op jit(solution)/shard_map/ppermute | solution.py:357
  791.1 8.2 copy-start.2
  799.2 2.1 collective-permute-start.8
  801.4 3.4 copy-start.7
  803.3 10.1 %collective-permute-start.9 = (bf16[1,8,64,256]{3,2,1,0:T(8,128)(2,1)}, bf16[1,8,64,256]{3,2,1,0:T(8,128)(2,1)}, u32[]{:S(2)}, u32[]{:S(2)}) collective-permute-start(bf16[1,8,64,256]{3,2,1,0:T(8,128)(2,1)} %add_convert_fusion), channel_id=1, source_target_pairs={{0,16},{8,24},{16,0},{24,8},{1,17},{9,25},{17,1},{25,9},{2,18},{10... | collective-permute-start | bytes 786440 | tf_op jit(solution)/shard_map/ppermute | solution.py:357
  804.8 7.7 copy-start.3
  804.8 7.7 copy-start.6
Sparse Core Ops, SparseCore 0:
  34.7 35.9 all-gather.2
  276.3 35.8 all-gather.4
  606.7 32.7 reduce-scatter.2
  642.0 31.4 reduce-scatter.4
